TPU v7x, 128 devices: a whole 4x4x4 slice. The times are simulated.
128 devices in a mesh: row: 8 (over x, core), col: 16 (over z, y).
Axes of the slice: x: 4, y: 4, z: 4, core: 2. Of those that a mesh axis runs over, the one named last changes fastest.
Arguments:
- tiles: bfloat16 [128, 64, 128, 128], P(('row', 'col')), may hold values from -6 to 6
- tile_mu: int32 [128], P(('row', 'col')), may hold values from 0 to 1
- tile_nu: int32 [128], P(('row', 'col')), may hold values from 0 to 7, as said below
- orbitals: bfloat16 [8192, 4096], P('row', 'col'), may hold values from -0.0625 to 0.0625
- metric_inverse: float32 [2, 64, 64], replicated, may hold values from -1 to 2, as said below
Outputs:
- fitted: bfloat16 [2, 64, 128, 4096], P(None, None, 'row', 'col')
- exchange: float32 [2, 128, 128], P(None, 'row')
Inputs may be any that keep to these rules, and one draw needn't show every extreme that they name: Within one grid row no two blocks have both the same tile_mu and the same tile_nu. `metric_inverse`: symmetric in its last two dimensions.
All inputs are finite; a program needn't handle non-finite values.
Results may differ from a plain program's by a relative error of at most 0.02.
Values may be sent and summed in bfloat16 or wider, within the bound.
No kernel may reach another device: no remote copies, remote signals or barrier semaphores. Data moves between devices by JAX's collectives and lax.ppermute only.
A program may use at most 192 MiB of HBM per device.

v0:
```python
import functools

import jax
import jax.numpy as jnp
from jax import lax
from jax.experimental import pallas as pl
from jax.experimental.pallas import tpu as pltpu
from jax.sharding import PartitionSpec as P

F32 = jnp.float32
BF16 = jnp.bfloat16

CHUNKS = (8, 8)

VMEM = pl.BlockSpec(memory_space=pltpu.VMEM)
SMEM = pl.BlockSpec(memory_space=pltpu.SMEM)
ANY = pl.BlockSpec(memory_space=pl.ANY)


def index(x, k, z, y):
    return ((x * 2 + k) * 4 + z) * 4 + y


def move(value, axis, step):
    pairs = []
    for x in range(4):
        for k in range(2):
            for z in range(4):
                for y in range(4):
                    to = dict(x=x, z=z, y=y)
                    to[axis] = (to[axis] + step * (1 - 2 * k)) % 4
                    pairs.append((index(x, k, z, y), index(to["x"], k, to["z"], to["y"])))
    return lax.ppermute(value, ("row", "col"), pairs)


def swap_core(value):
    return lax.ppermute(value, "row", [(r, r ^ 1) for r in range(8)])


def call(body, out_shape, in_specs, name, args, after=(), scratch=(), flops=0, nbytes=0, limit=8):
    given, marks = len(args), [mark(item) for item in after]

    def kernel(*refs):
        body(*refs[:given], *refs[given + len(marks):])

    return pl.pallas_call(
        kernel,
        out_shape=out_shape,
        in_specs=list(in_specs) + [VMEM] * len(marks),
        out_specs=jax.tree.map(lambda _: VMEM, out_shape),
        scratch_shapes=list(scratch),
        name=name,
        compiler_params=pltpu.CompilerParams(vmem_limit_bytes=limit * 1024 * 1024),
        cost_estimate=pl.CostEstimate(flops=flops, bytes_accessed=nbytes, transcendentals=0),
    )(*args, *marks)


def mark(item):
    item = item[(0,) * (item.ndim - 2)]
    return item[:16, :128]


def copy_body(source, out):
    out[...] = source[...]


def gate(value, after):
    shape = jax.ShapeDtypeStruct(value.shape, value.dtype)
    return call(copy_body, shape, [VMEM], "gate", (value,), after, nbytes=2 * value.size * 2)


def relayout_body(parts, yc_ref, x_ref, *refs):
    *orbitals, out, wide = refs
    wide[...] = x_ref[...].reshape(wide.shape).astype(F32)
    row = 0
    for offset, count in parts:
        for r in [2 * x + k for k in range(2) for x in range(4)]:
            for u in range(16 * r + offset, 16 * r + offset + count):
                out[0, row] = wide[pl.ds(u, 16, stride=128), :].astype(BF16)
                row += 1
        out[0, row] = jnp.full((16, 128), yc_ref[2].astype(F32), F32).astype(BF16)
        row += 1
    for ref in orbitals:
        for half in range(2):
            out[0, row:row + 64] = ref[:, half * 128:(half + 1) * 128].reshape(64, 16, 128)
            row += 64


def relayout(tile, yc, parts, orbitals):
    def block(step, yc_ref):
        return ((yc_ref[0] + step * yc_ref[1] + 4) % 4, 0, 0)

    blocks = sum(8 * count + 1 for _, count in parts) + 128 * len(orbitals)
    return pl.pallas_call(
        functools.partial(relayout_body, parts),
        grid_spec=pltpu.PrefetchScalarGridSpec(
            num_scalar_prefetch=1,
            grid=(4,),
            in_specs=[pl.BlockSpec((16, 128, 128), block)] + [VMEM] * len(orbitals),
            out_specs=pl.BlockSpec((1, blocks, 16, 128), lambda step, yc_ref: (step, 0, 0, 0)),
            scratch_shapes=[pltpu.VMEM((2048, 128), F32)],
        ),
        out_shape=jax.ShapeDtypeStruct((4, blocks, 16, 128), BF16),
        name="relayout",
        compiler_params=pltpu.CompilerParams(vmem_limit_bytes=8 * 1024 * 1024),
        cost_estimate=pl.CostEstimate(flops=0, bytes_accessed=4 << 20, transcendentals=0),
    )(yc, tile, *orbitals)


def stack_body(start, first, a, b, c, out):
    blocks = out.shape[1] // 16
    out[0] = first[0, start:start + blocks].reshape(out.shape[1:])
    for i, ref in enumerate((a, b, c)):
        out[i + 1] = ref[start:start + blocks].reshape(out.shape[1:])


def product_body(count, xky_ref, t0, t1, t2, t3, orb, o1, o2, o3, own, peer, rows, orbs):
    rp = 16 * count
    x, k, sign = xky_ref[0], xky_ref[1], xky_ref[2]
    for ref in (t0, t1, t2, t3):
        for i in range(4):
            code = jnp.max(ref[i, 8 * rp:8 * rp + 16, :].astype(F32)).astype(jnp.int32)
            m = code >> 3
            lane = pl.multiple_of((code & 7) * 128, 128)
            for h in range(2):
                for e in range(4):
                    towards = (x + sign * e + 4) % 4 if h == 0 else (x - sign * e + 4) % 4
                    source = pl.multiple_of((((k + h) % 2) * 4 + towards) * rp, rp)
                    place = (h * 4 + e) * rp
                    rows[m, place:place + rp, pl.ds(lane, 128)] = ref[i, pl.ds(source, rp), :]
    orbs[0] = orb[...]
    for d, ref in enumerate((o1, o2, o3)):
        for half in range(2):
            start = ref.shape[0] - 128 + 64 * half
            orbs[d + 1, :, half * 128:(half + 1) * 128] = ref[start:start + 64].reshape(1024, 128)
    for h, out in ((1, peer), (0, own)):
        for d in range(4):
            orb = orbs[d]
            place = d if h == 0 else (4 - d) % 4
            for m in range(2):
                acc = jnp.dot(rows[m, h * 4 * rp:(h + 1) * 4 * rp, :], orb, preferred_element_type=F32)
                for e in range(4):
                    out[e, place, m] = acc[e * rp:(e + 1) * rp].astype(BF16)


def product(count, xky, tiles, orbs, after):
    rp = 16 * count
    shape = jax.ShapeDtypeStruct((4, 4, 2, rp, 256), BF16)
    return call(
        functools.partial(product_body, count),
        [shape, shape],
        [SMEM] + [VMEM] * 8,
        "product",
        (xky, *tiles, *orbs),
        after,
        scratch=[pltpu.VMEM((2, 8 * rp, 1024), BF16), pltpu.VMEM((4, 1024, 256), BF16)],
        flops=2 * 2 * 8 * rp * 1024 * 1024,
        nbytes=6 << 20,
        limit=14,
    )


def pair_body(a, b, *outs):
    for e, out in enumerate(outs):
        out[...] = (a[e + 1].astype(F32) + b[e + 1].astype(F32)).astype(BF16)


def total_body(a, b, j1, j2, j3, *outs):
    for d, out in enumerate(outs):
        value = a[0, d].astype(F32) + b[0, d].astype(F32)
        value = value + j1[d].astype(F32) + j2[d].astype(F32) + j3[d].astype(F32)
        out[...] = value.astype(BF16)


def fit_body(count, xky_ref, c0, c1, c2, c3, metric, fitted, s0, s1, s2, s3, coef, fit):
    x, k, sign, y = xky_ref[0], xky_ref[1], xky_ref[2], xky_ref[3]
    for d, ref in enumerate((c0, c1, c2, c3)):
        row = pl.multiple_of(((y + sign * d + 4) % 4) * 16, 16)
        for m in range(2):
            for uu in range(count):
                coef[m, pl.ds(row, 16), uu * 256:(uu + 1) * 256] = ref[m, uu * 16:(uu + 1) * 16, :]
    for m in range(2):
        high = metric[m].astype(BF16)
        low = (metric[m] - high.astype(F32)).astype(BF16)
        both = jnp.concatenate([high, low], axis=1)
        value = coef[m]
        fit[m] = jnp.dot(both, jnp.concatenate([value, value], axis=0), preferred_element_type=F32).astype(BF16)
    fitted[...] = fit[...]
    for e, out in enumerate((s0, s1, s2, s3)):
        for h in range(2):
            m = (k + h) % 2
            q = pl.multiple_of(((x + sign * e + 4) % 4) * 16, 16)
            out[h, 0] = fit[m, pl.ds(q, 16), :]
            out[h, 1] = coef[m, pl.ds(q, 16), :]


def fit_part(count, xky, pieces, metric, after):
    lanes = 256 * count
    shape = jax.ShapeDtypeStruct((2, 64, lanes), BF16)
    send = jax.ShapeDtypeStruct((2, 2, 16, lanes), BF16)
    return call(
        functools.partial(fit_body, count),
        [shape, send, send, send, send],
        [SMEM] + [VMEM] * 5,
        "fit",
        (xky, *pieces, metric),
        after,
        scratch=[pltpu.VMEM((2, 64, lanes), BF16), pltpu.VMEM((2, 64, lanes), BF16)],
        flops=2 * 2 * 64 * 128 * lanes,
        nbytes=1 << 20,
    )


def assemble_body(parts, *refs):
    out = refs[-1]
    for (offset, count), ref in zip(parts, refs[:-1]):
        for uu in range(count):
            for m in range(2):
                out[m, :, offset + uu, :] = ref[m, :, uu * 256:(uu + 1) * 256]


def exchange_body(parts, xk_ref, *refs):
    *outs, total = refs[-9:-4]
    wides = refs[-4:]
    x, k, sign = xk_ref[0], xk_ref[1], xk_ref[2]
    refs = refs[:-9]
    for part, (offset, count) in enumerate(parts):
        near = refs[5 * part:5 * part + 4]
        far = refs[5 * part + 4]
        for e in range(4):
            for h in range(2):
                source = (x - sign * e + 4) % 4 if h == 0 else (x + sign * e + 4) % 4
                r = 2 * source + (k + h) % 2
                for uu in range(count):
                    row = pl.multiple_of((16 * r + offset + uu) * 16, 16)
                    for index, wide in enumerate(wides):
                        which, lane = index // 2, uu * 256 + index % 2 * 128
                        lanes = slice(lane, lane + 128)
                        value = near[e][0, which, :, lanes] if h == 0 else far[e, which, :, lanes]
                        wide[pl.ds(row, 16), :] = value.astype(F32)
    acc = jnp.zeros((128, 128), F32)
    for q in range(16):
        halves = [wide[pl.ds(q, 128, stride=16), :].astype(BF16) for wide in wides]
        a = jnp.concatenate(halves[:2], axis=1)
        b = jnp.concatenate(halves[2:], axis=1)
        acc = acc + lax.dot_general(a, b, (((1,), (1,)), ((), ())), preferred_element_type=F32)
    total[...] = acc
    for e, out in enumerate(outs):
        out[...] = total[pl.ds(pl.multiple_of(((x + sign * e + 4) % 4) * 32, 32), 32), :]


def on_device(tiles, tile_mu, tile_nu, orbitals, metric_inverse):
    row = lax.axis_index("row").astype(jnp.int32)
    col = lax.axis_index("col").astype(jnp.int32)
    x, k, y = row // 2, row % 2, col % 4
    sign = 1 - 2 * k
    xk = jnp.stack([x, k, sign])
    xky = jnp.stack([x, k, sign, y])
    yc = jnp.stack([y, sign, tile_mu[0] * 8 + tile_nu[0]])
    last = len(CHUNKS) - 1
    offsets = [sum(CHUNKS[:i]) for i in range(len(CHUNKS))]
    parts = list(zip(offsets, CHUNKS))

    shards, gathered, sums, fits = {}, {}, {}, {}
    groups = [parts[:1], parts[1:]]
    spread = []

    def over_y(group, held):
        with jax.named_scope("tiles_over_y"):
            spread.append((held, *[move(held[d], "y", d) for d in (1, 2, 3)]))

    def stack(i, after):
        with jax.named_scope("tiles_over_z"):
            start = 8 * (parts[i][0] - parts[min(i, 1)][0]) + max(i - 1, 0)
            shape = jax.ShapeDtypeStruct((4, (8 * parts[i][1] + 1) * 16, 128), BF16)
            body = functools.partial(stack_body, start)
            shards[i] = call(body, shape, [VMEM] * 4, "stack", spread[min(i, 1)], after, nbytes=1 << 20)

    def gather_z(i, after):
        with jax.named_scope("tiles_over_z"):
            near = gate(move(shards[i], "z", 1), after)
            across = move(gate(shards[i], [near]), "z", 3)
            gathered[i] = (shards[i], near, across, move(near, "z", 1))

    partial, got, blocks, arrived, pieces = {}, {}, {}, {}, {}

    def multiply(i, after):
        with jax.named_scope("products"):
            partial[i] = product(CHUNKS[i], xky, gathered[i], orbs, after)

    def sum_rows(i, after):
        mine, others = partial[i]
        others = gate(others, after) if after else others
        with jax.named_scope("sum_cores"):
            twin = swap_core(others)
            shape = jax.ShapeDtypeStruct(mine.shape[1:], BF16)
            sends = call(pair_body, [shape] * 3, [VMEM] * 2, "pair", (mine, twin), nbytes=3 << 20)
        with jax.named_scope("sum_x"):
            got[i] = (mine, twin, *[move(send, "x", e + 1) for e, send in enumerate(sends)])

    def coeffs(i):
        with jax.named_scope("sum_x"):
            shape = jax.ShapeDtypeStruct(got[i][0].shape[2:], BF16)
            blocks[i] = call(total_body, [shape] * 4, [VMEM] * 5, "total", got[i], nbytes=2 << 20)
        with jax.named_scope("coeffs_over_y"):
            blocks[i] = [blocks[i][0]] + [move(blocks[i][d], "y", -d) for d in (1, 2, 3)]

    def fit(i, after):
        with jax.named_scope("fit"):
            fits[i], *sends = fit_part(CHUNKS[i], xky, blocks[i], metric_inverse, after)
        with jax.named_scope("exchange_over_row"):
            arrived[i] = [sends[0]] + [move(sends[e], "x", e) for e in (1, 2, 3)]
            pieces[i] = arrived[i] + [swap_core(jnp.stack([part[1] for part in arrived[i]]))]

    laid = [relayout(tiles[0], yc, group, held) for group, held in zip(groups, ([], [orbitals]))]
    over_y(groups[0], laid[0])
    stack(0, [laid[1]])
    over_y(groups[1], gate(laid[1], [shards[0]]))
    gather_z(0, [spread[1][3]])
    orbs = [orbitals, *spread[1][1:]]
    for i in range(last + 1):
        if i < last:
            stack(i + 1, gathered[i][2:])
        multiply(i, ([shards[i + 1]] if i < last else []) + (list(got[i - 1][2:4]) if i > 0 else []))
        if i < last:
            gather_z(i + 1, [partial[i][0]])
        sum_rows(i, [gathered[i + 1][1]] if i < last else [])
        if i == 0:
            coeffs(0)
        else:
            coeffs(i)
            fit(i - 1, [blocks[i][0]])
    fit(last, arrived[last - 1][1:3] if last else [])

    with jax.named_scope("fitted_out"):
        fitted = call(
            functools.partial(assemble_body, parts),
            jax.ShapeDtypeStruct((2, 64, 16, 256), BF16),
            [VMEM] * len(parts),
            "assemble",
            [fits[i] for i in range(last + 1)],
            nbytes=2 << 20,
        )

    with jax.named_scope("exchange"):
        pieces = [piece for i in range(last + 1) for piece in pieces[i]]
        blocks = call(
            functools.partial(exchange_body, parts),
            [jax.ShapeDtypeStruct((32, 128), F32)] * 4,
            [SMEM] + [VMEM] * len(pieces),
            "exchange",
            (xk, *pieces),
            scratch=[pltpu.VMEM((128, 128), F32)] + [pltpu.VMEM((2048, 128), F32)] * 4,
            flops=2 * 128 * 128 * 4096,
            nbytes=2 << 20,
        )
        total = blocks[0] + (move(blocks[1], "x", 1) + move(blocks[2], "x", 2) + move(blocks[3], "x", 3))
        keep = jnp.where(k == 0, total[:16], total[16:])
        got = swap_core(jnp.where(k == 0, total[16:], total[:16]))
        total = jnp.stack([jnp.where(k == 0, keep, got), jnp.where(k == 0, got, keep)])
        for axis in ("y", "z"):
            total = total + (move(total, axis, 1) + move(total, axis, 2) + move(total, axis, 3))
        exchange = total / 262144.0
    return fitted, exchange


def solution(mesh):
    return jax.shard_map(
        on_device,
        mesh=mesh,
        in_specs=(
            P(("row", "col"), None, None, None),
            P(("row", "col")),
            P(("row", "col")),
            P("row", "col"),
            P(),
        ),
        out_specs=(P(None, None, "row", "col"), P(None, "row", None)),
        check_vma=False,
    )
```

profile of v0, /device:TPU:6, one launch (start us, length us, event | category | flops | bytes accessed | tf_op | source)
XLA Modules:
  0.0 220.5 jit_solution(7388880210696358068)
XLA Ops:
  2.0 1.6 copy-done
  3.6 1.9 relayout.2.refs_0_
  5.7 1.6 collective-permute-start
  7.4 2.9 %collective-permute-start.1 = (bf16[65,16,128]{2,1,0:T(8,128)(2,1)S(1)}, bf16[65,16,128]{2,1,0:T(8,128)(2,1)S(1)}, u32[]{:S(2)}, u32[]{:S(2)}) collective-permute-start(bf16[65,16,128]{2,1,0:T(8,128)(2,1)S(1)} %get-tuple-element.70), channel_id=1, source_target_pairs={{0,2},{1,3},{2,0},{3,1},{4,6},{5,7},{6,4},{7,5},{8,10},{9,11},{10,... | collective-permute-start | bytes 798728 | tf_op jit(solution)/shard_map/tiles_over_y/ppermute | solution.py:33
  10.3 1.3 collective-permute-start.2
  11.6 2.3 %relayout.3.refs_0_ = bf16[4,193,16,128]{3,2,1,0:T(8,128)(2,1)S(1)} custom-call(s32[3]{0:T(128)S(1)} %pad_add_fusion.1.yc_ref, bf16[64,128,128]{2,1,0:T(8,128)(2,1)S(1)} %bitcast.50, bf16[1024,256]{1,0:T(8,128)(2,1)S(1)} %copy-done.10), custom_call_target="tpu_custom_call" | custom-call | bytes 4194304 | tf_op jit(solution)/shard_map/relayout/pallas_call | solution.py:94
  13.9 2.2 collective-permute-done.refs_1_
  16.1 6.5 %collective-permute-done.1.refs_2_ = bf16[65,16,128]{2,1,0:T(8,128)(2,1)S(1)} collective-permute-done((bf16[65,16,128]{2,1,0:T(8,128)(2,1)S(1)}, bf16[65,16,128]{2,1,0:T(8,128)(2,1)S(1)}, u32[]{:S(2)}, u32[]{:S(2)}) %collective-permute-start.1) | collective-permute-done | bytes 266272 | tf_op jit(solution)/shard_map/tiles_over_y/ppermute | solution.py:33
  22.7 2.0 collective-permute-start.3
  25.3 1.3 collective-permute-start.4
  26.6 10.8 %collective-permute-done.4.refs_3_.refs_8_ = bf16[193,16,128]{2,1,0:T(8,128)(2,1)S(1)} collective-permute-done((bf16[193,16,128]{2,1,0:T(8,128)(2,1)S(1)}, bf16[193,16,128]{2,1,0:T(8,128)(2,1)S(1)}, u32[]{:S(2)}, u32[]{:S(2)}) %collective-permute-start.4) | collective-permute-done | bytes 790560 | tf_op jit(solution)/shard_map/tiles_over_y/ppermute | solution.py:33
  37.4 2.3 %collective-permute-done.3.refs_0_ = bf16[4,1040,128]{2,1,0:T(8,128)(2,1)S(1)} collective-permute-done((bf16[4,1040,128]{2,1,0:T(8,128)(2,1)S(1)}, bf16[4,1040,128]{2,1,0:T(8,128)(2,1)S(1)}, u32[]{:S(2)}, u32[]{:S(2)}) %collective-permute-start.3) | collective-permute-done | bytes 1064992 | tf_op jit(solution)/shard_map/tiles_over_z/ppermute | solution.py:33
  39.9 2.1 collective-permute-start.5
  42.0 2.7 %collective-permute-start.8 = (bf16[193,16,128]{2,1,0:T(8,128)(2,1)S(1)}, bf16[193,16,128]{2,1,0:T(8,128)(2,1)S(1)}, u32[]{:S(2)}, u32[]{:S(2)}) collective-permute-start(bf16[193,16,128]{2,1,0:T(8,128)(2,1)S(1)} %get-tuple-element.66), channel_id=1, source_target_pairs={{0,2},{1,3},{2,0},{3,1},{4,6},{5,7},{6,4},{7,5},{8,10},{9,11},{10,... | collective-permute-start | bytes 2371592 | tf_op jit(solution)/shard_map/tiles_over_y/ppermute | solution.py:33
  44.7 19.9 %collective-permute-done.5.refs_3_ = bf16[4,1040,128]{2,1,0:T(8,128)(2,1)S(1)} collective-permute-done((bf16[4,1040,128]{2,1,0:T(8,128)(2,1)S(1)}, bf16[4,1040,128]{2,1,0:T(8,128)(2,1)S(1)}, u32[]{:S(2)}, u32[]{:S(2)}) %collective-permute-start.5) | collective-permute-done | bytes 1064992 | tf_op jit(solution)/shard_map/tiles_over_z/ppermute | solution.py:33
  65.3 6.9 %collective-permute-done.7.refs_1_.refs_6_ = bf16[193,16,128]{2,1,0:T(8,128)(2,1)S(1)} collective-permute-done((bf16[193,16,128]{2,1,0:T(8,128)(2,1)S(1)}, bf16[193,16,128]{2,1,0:T(8,128)(2,1)S(1)}, u32[]{:S(2)}, u32[]{:S(2)}) %collective-permute-start.7) | collective-permute-done | bytes 790560 | tf_op jit(solution)/shard_map/tiles_over_y/ppermute | solution.py:33
  77.9 1.2 copy-done.14
  79.1 1.2 copy-done.16
  80.3 6.5 %product.2 = (bf16[4,4,2,128,256]{4,3,2,1,0:T(8,128)(2,1)S(1)}, bf16[4,4,2,128,256]{4,3,2,1,0:T(8,128)(2,1)S(1)}) custom-call(s32[4]{0:T(128)S(1)} %pad_add_fusion.refs_0_, bf16[4,1040,128]{2,1,0:T(8,128)(2,1)S(1)} %stack.56.refs_0_.refs_1_, bf16[4,1040,128]{2,1,0:T(8,128)(2,1)S(1)} %gate.7.refs_2_, bf16[4,1040,128]{2,1,0:T(8,128)(2,1)S(1)} %copy-done.14, ...), custom_call_target="tpu_custom_call" | custom-call | flops 4294967296 | bytes 6291456 | tf_op jit(solution)/shard_map/products/product/pallas_call | solution.py:46
  86.9 2.7 %collective-permute-done.9.refs_0_ = bf16[4,1040,128]{2,1,0:T(8,128)(2,1)} collective-permute-done((bf16[4,1040,128]{2,1,0:T(8,128)(2,1)S(1)}, bf16[4,1040,128]{2,1,0:T(8,128)(2,1)}, u32[]{:S(2)}, u32[]{:S(2)}) %collective-permute-start.9) | collective-permute-done | bytes 1064992 | tf_op jit(solution)/shard_map/tiles_over_z/ppermute | solution.py:33
  89.6 1.3 gate.9.refs_2_
  93.4 1.9 collective-permute-done.10.refs_1_
  96.2 2.4 %collective-permute-start.12 = (bf16[4,2,128,256]{3,2,1,0:T(8,128)(2,1)S(1)}, bf16[4,2,128,256]{3,2,1,0:T(8,128)(2,1)S(1)}, u32[]{:S(2)}, u32[]{:S(2)}) collective-permute-start(bf16[4,2,128,256]{3,2,1,0:T(8,128)(2,1)S(1)} %get-tuple-element.37), channel_id=1, source_target_pairs={{0,64},{1,65},{2,66},{3,67},{4,68},{5,69},{6,70},{7,71},{8,72},{9,... | collective-permute-start | bytes 1572872 | tf_op jit(solution)/shard_map/sum_x/ppermute | solution.py:33
  98.7 11.0 %collective-permute-done.11.refs_2_ = bf16[4,2,128,256]{3,2,1,0:T(8,128)(2,1)S(1)} collective-permute-done((bf16[4,2,128,256]{3,2,1,0:T(8,128)(2,1)S(1)}, bf16[4,2,128,256]{3,2,1,0:T(8,128)(2,1)S(1)}, u32[]{:S(2)}, u32[]{:S(2)}) %collective-permute-start.11) | collective-permute-done | bytes 524320 | tf_op jit(solution)/shard_map/sum_x/ppermute | solution.py:33
  109.6 3.1 %collective-permute-done.12.refs_3_ = bf16[4,2,128,256]{3,2,1,0:T(8,128)(2,1)S(1)} collective-permute-done((bf16[4,2,128,256]{3,2,1,0:T(8,128)(2,1)S(1)}, bf16[4,2,128,256]{3,2,1,0:T(8,128)(2,1)S(1)}, u32[]{:S(2)}, u32[]{:S(2)}) %collective-permute-start.12) | collective-permute-done | bytes 524320 | tf_op jit(solution)/shard_map/sum_x/ppermute | solution.py:33
  112.7 4.8 %collective-permute-done.17.refs_3_ = bf16[4,1040,128]{2,1,0:T(8,128)(2,1)S(1)} collective-permute-done((bf16[4,1040,128]{2,1,0:T(8,128)(2,1)S(1)}, bf16[4,1040,128]{2,1,0:T(8,128)(2,1)S(1)}, u32[]{:S(2)}, u32[]{:S(2)}) %collective-permute-start.17) | collective-permute-done | bytes 1064992 | tf_op jit(solution)/shard_map/tiles_over_z/ppermute | solution.py:33
  118.5 6.5 %product.3 = (bf16[4,4,2,128,256]{4,3,2,1,0:T(8,128)(2,1)S(1)}, bf16[4,4,2,128,256]{4,3,2,1,0:T(8,128)(2,1)S(1)}) custom-call(s32[4]{0:T(128)S(1)} %pad_add_fusion.refs_0_, bf16[4,1040,128]{2,1,0:T(8,128)(2,1)S(1)} %stack.57.refs_0_.refs_1_, bf16[4,1040,128]{2,1,0:T(8,128)(2,1)S(1)} %gate.9.refs_2_, ...), custom_call_target="tpu_custom_call" | custom-call | flops 4294967296 | bytes 6291456 | tf_op jit(solution)/shard_map/products/product/pallas_call | solution.py:46
  126.0 3.3 %collective-permute-done.19.refs_1_ = bf16[4,4,2,128,256]{4,3,2,1,0:T(8,128)(2,1)S(1)} collective-permute-done((bf16[4,4,2,128,256]{4,3,2,1,0:T(8,128)(2,1)S(1)}, bf16[4,4,2,128,256]{4,3,2,1,0:T(8,128)(2,1)S(1)}, u32[]{:S(2)}, u32[]{:S(2)}) %collective-permute-start.19) | collective-permute-done | bytes 2097184 | tf_op jit(solution)/shard_map/sum_cores/ppermute | solution.py:37
  130.2 2.4 %collective-permute-start.21 = (bf16[4,2,128,256]{3,2,1,0:T(8,128)(2,1)S(1)}, bf16[4,2,128,256]{3,2,1,0:T(8,128)(2,1)S(1)}, u32[]{:S(2)}, u32[]{:S(2)}) collective-permute-start(bf16[4,2,128,256]{3,2,1,0:T(8,128)(2,1)S(1)} %get-tuple-element.46), channel_id=1, source_target_pairs={{0,64},{1,65},{2,66},{3,67},{4,68},{5,69},{6,70},{7,71},{8,72},{9,... | collective-permute-start | bytes 1572872 | tf_op jit(solution)/shard_map/sum_x/ppermute | solution.py:33
  132.6 6.2 %collective-permute-done.13.refs_4_ = bf16[4,2,128,256]{3,2,1,0:T(8,128)(2,1)S(1)} collective-permute-done((bf16[4,2,128,256]{3,2,1,0:T(8,128)(2,1)S(1)}, bf16[4,2,128,256]{3,2,1,0:T(8,128)(2,1)S(1)}, u32[]{:S(2)}, u32[]{:S(2)}) %collective-permute-start.13) | collective-permute-done | bytes 524320 | tf_op jit(solution)/shard_map/sum_x/ppermute | solution.py:33
  139.3 10.8 %collective-permute-done.20.refs_2_ = bf16[4,2,128,256]{3,2,1,0:T(8,128)(2,1)S(1)} collective-permute-done((bf16[4,2,128,256]{3,2,1,0:T(8,128)(2,1)S(1)}, bf16[4,2,128,256]{3,2,1,0:T(8,128)(2,1)S(1)}, u32[]{:S(2)}, u32[]{:S(2)}) %collective-permute-start.20) | collective-permute-done | bytes 524320 | tf_op jit(solution)/shard_map/sum_x/ppermute | solution.py:33
  150.0 8.0 %collective-permute-done.22.refs_4_ = bf16[4,2,128,256]{3,2,1,0:T(8,128)(2,1)S(1)} collective-permute-done((bf16[4,2,128,256]{3,2,1,0:T(8,128)(2,1)S(1)}, bf16[4,2,128,256]{3,2,1,0:T(8,128)(2,1)S(1)}, u32[]{:S(2)}, u32[]{:S(2)}) %collective-permute-start.22) | collective-permute-done | bytes 524320 | tf_op jit(solution)/shard_map/sum_x/ppermute | solution.py:33
  159.4 2.0 collective-permute-start.26
  163.4 3.6 %collective-permute-start.27 = (bf16[2,2,16,2048]{3,2,1,0:T(8,128)(2,1)S(1)}, bf16[2,2,16,2048]{3,2,1,0:T(8,128)(2,1)S(1)}, u32[]{:S(2)}, u32[]{:S(2)}) collective-permute-start(bf16[2,2,16,2048]{3,2,1,0:T(8,128)(2,1)S(1)} %get-tuple-element.54), channel_id=1, source_target_pairs={{0,64},{1,65},{2,66},{3,67},{4,68},{5,69},{6,70},{7,71},{8,72},{9,... | collective-permute-start | bytes 786440 | tf_op jit(solution)/shard_map/exchange_over_row/ppermute | solution.py:33
  167.2 8.0 %collective-permute-start.28 = (bf16[2,2,16,2048]{3,2,1,0:T(8,128)(2,1)S(1)}, bf16[2,2,16,2048]{3,2,1,0:T(8,128)(2,1)S(1)}, u32[]{:S(2)}, u32[]{:S(2)}) collective-permute-start(bf16[2,2,16,2048]{3,2,1,0:T(8,128)(2,1)S(1)} %get-tuple-element.57), channel_id=1, source_target_pairs={{0,96},{1,97},{2,98},{3,99},{4,100},{5,101},{6,102},{7,103},{8,104... | collective-permute-start | bytes 786440 | tf_op jit(solution)/shard_map/exchange_over_row/ppermute | solution.py:33
  177.2 2.5 %collective-permute-start.30 = (bf16[2,2,16,2048]{3,2,1,0:T(8,128)(2,1)S(1)}, bf16[2,2,16,2048]{3,2,1,0:T(8,128)(2,1)S(1)}, u32[]{:S(2)}, u32[]{:S(2)}) collective-permute-start(bf16[2,2,16,2048]{3,2,1,0:T(8,128)(2,1)S(1)} %get-tuple-element.59), channel_id=1, source_target_pairs={{0,32},{1,33},{2,34},{3,35},{4,36},{5,37},{6,38},{7,39},{8,40},{9,... | collective-permute-start | bytes 786440 | tf_op jit(solution)/shard_map/exchange_over_row/ppermute | solution.py:33
  179.7 2.0 collective-permute-done.28.refs_4_
  181.9 9.4 %collective-permute-done.32.refs_9_ = bf16[2,2,16,2048]{3,2,1,0:T(8,128)(2,1)S(1)} collective-permute-done((bf16[2,2,16,2048]{3,2,1,0:T(8,128)(2,1)S(1)}, bf16[2,2,16,2048]{3,2,1,0:T(8,128)(2,1)S(1)}, u32[]{:S(2)}, u32[]{:S(2)}) %collective-permute-start.32) | collective-permute-done | bytes 262176 | tf_op jit(solution)/shard_map/exchange_over_row/ppermute | solution.py:33
  191.6 1.8 collective-permute-done.33.refs_10_
  193.4 2.0 exchange.1
  195.5 3.2 %collective-permute-start.34 = (f32[32,128]{1,0:T(8,128)S(1)}, f32[32,128]{1,0:T(8,128)S(1)}, u32[]{:S(2)}, u32[]{:S(2)}) collective-permute-start(f32[32,128]{1,0:T(8,128)S(1)} %get-tuple-element.63), channel_id=1, source_target_pairs={{0,32},{1,33},{2,34},{3,35},{4,36},{5,37},{6,38},{7,39},{8,40},{9,... | collective-permute-start | bytes 49160 | tf_op jit(solution)/shard_map/exchange/ppermute | solution.py:33
  198.8 1.8 collective-permute-start.35
  200.6 3.4 %collective-permute-done.35 = f32[32,128]{1,0:T(8,128)S(1)} collective-permute-done((f32[32,128]{1,0:T(8,128)S(1)}, f32[32,128]{1,0:T(8,128)S(1)}, u32[]{:S(2)}, u32[]{:S(2)}) %collective-permute-start.35) | collective-permute-done | bytes 16416 | tf_op jit(solution)/shard_map/exchange/ppermute | solution.py:33
  207.4 3.1 %collective-permute-start.39 = (f32[2,16,128]{2,1,0:T(8,128)S(1)}, f32[2,16,128]{2,1,0:T(8,128)S(1)}, u32[]{:S(2)}, u32[]{:S(2)}) collective-permute-start(f32[2,16,128]{2,1,0:T(8,128)S(1)} %pad_maximum_fusion.2), channel_id=1, source_target_pairs={{0,2},{1,3},{2,0},{3,1},{4,6},{5,7},{6,4},{7,5},{8,10},{9,11},{10,... | collective-permute-start | bytes 49160 | tf_op jit(solution)/shard_map/exchange/ppermute | solution.py:33
  211.3 1.3 collective-permute-done.39
  213.1 1.6 collective-permute-start.41
  214.7 2.7 %collective-permute-start.42 = (f32[2,16,128]{2,1,0:T(8,128)S(1)}, f32[2,16,128]{2,1,0:T(8,128)S(1)}, u32[]{:S(2)}, u32[]{:S(2)}) collective-permute-start(f32[2,16,128]{2,1,0:T(8,128)S(1)} %add_add_fusion), channel_id=1, source_target_pairs={{0,8},{1,9},{2,10},{3,11},{4,12},{5,13},{6,14},{7,15},{8,0},{9,1},... | collective-permute-start | bytes 49160 | tf_op jit(solution)/shard_map/exchange/ppermute | solution.py:33
  217.3 2.5 %assemble.1 = bf16[2,64,16,256]{3,2,1,0:T(8,128)(2,1)} custom-call(bf16[2,64,2048]{2,1,0:T(8,128)(2,1)S(1)} %get-tuple-element.49.refs_0_, bf16[2,64,2048]{2,1,0:T(8,128)(2,1)S(1)} %get-tuple-element.55.refs_1_), custom_call_target="tpu_custom_call" | custom-call | bytes 2097152 | tf_op jit(solution)/shard_map/fitted_out/assemble/pallas_call | solution.py:46
  (135 shorter events, 25.4 us)
Async XLA Ops:
  5.7 10.4 %collective-permute-start = (bf16[65,16,128]{2,1,0:T(8,128)(2,1)S(1)}, bf16[65,16,128]{2,1,0:T(8,128)(2,1)S(1)}, u32[]{:S(2)}, u32[]{:S(2)}) collective-permute-start(bf16[65,16,128]{2,1,0:T(8,128)(2,1)S(1)} %get-tuple-element.71), channel_id=1, source_target_pairs={{0,1},{1,2},{2,3},{3,0},{4,5},{5,6},{6,7},{7,4},{8,9},{9,10},{10,1... | collective-permute-start | bytes 798728 | tf_op jit(solution)/shard_map/tiles_over_y/ppermute | solution.py:33
  7.4 15.2 %collective-permute-start.1 = (bf16[65,16,128]{2,1,0:T(8,128)(2,1)S(1)}, bf16[65,16,128]{2,1,0:T(8,128)(2,1)S(1)}, u32[]{:S(2)}, u32[]{:S(2)}) collective-permute-start(bf16[65,16,128]{2,1,0:T(8,128)(2,1)S(1)} %get-tuple-element.70), channel_id=1, source_target_pairs={{0,2},{1,3},{2,0},{3,1},{4,6},{5,7},{6,4},{7,5},{8,10},{9,11},{10,... | collective-permute-start | bytes 798728 | tf_op jit(solution)/shard_map/tiles_over_y/ppermute | solution.py:33
  10.3 12.3 %collective-permute-start.2 = (bf16[65,16,128]{2,1,0:T(8,128)(2,1)S(1)}, bf16[65,16,128]{2,1,0:T(8,128)(2,1)S(1)}, u32[]{:S(2)}, u32[]{:S(2)}) collective-permute-start(bf16[65,16,128]{2,1,0:T(8,128)(2,1)S(1)} %get-tuple-element.69), channel_id=1, source_target_pairs={{0,3},{1,0},{2,1},{3,2},{4,7},{5,4},{6,5},{7,6},{8,11},{9,8},{10,9... | collective-permute-start | bytes 798728 | tf_op jit(solution)/shard_map/tiles_over_y/ppermute | solution.py:33
  22.7 17.1 %collective-permute-start.3 = (bf16[4,1040,128]{2,1,0:T(8,128)(2,1)S(1)}, bf16[4,1040,128]{2,1,0:T(8,128)(2,1)S(1)}, u32[]{:S(2)}, u32[]{:S(2)}) collective-permute-start(bf16[4,1040,128]{2,1,0:T(8,128)(2,1)S(1)} %stack.56.refs_0_.refs_1_), channel_id=1, source_target_pairs={{0,4},{1,5},{2,6},{3,7},{4,8},{5,9},{6,10},{7,11},{8,12},{9,13},{1... | collective-permute-start | bytes 3194888 | tf_op jit(solution)/shard_map/tiles_over_z/ppermute | solution.py:33
  25.3 12.1 %collective-permute-start.4 = (bf16[193,16,128]{2,1,0:T(8,128)(2,1)S(1)}, bf16[193,16,128]{2,1,0:T(8,128)(2,1)S(1)}, u32[]{:S(2)}, u32[]{:S(2)}) collective-permute-start(bf16[193,16,128]{2,1,0:T(8,128)(2,1)S(1)} %get-tuple-element.68), channel_id=1, source_target_pairs={{0,3},{1,0},{2,1},{3,2},{4,7},{5,4},{6,5},{7,6},{8,11},{9,8},{10,9... | collective-permute-start | bytes 2371592 | tf_op jit(solution)/shard_map/tiles_over_y/ppermute | solution.py:33
  37.4 34.8 %copy-start.2 = (bf16[193,16,128]{2,1,0:T(8,128)(2,1)}, bf16[193,16,128]{2,1,0:T(8,128)(2,1)S(1)}, u32[]{:S(2)}) copy-start(bf16[193,16,128]{2,1,0:T(8,128)(2,1)S(1)} %collective-permute-done.4.refs_3_.refs_8_) | copy-start | bytes 2371588
  39.9 24.6 %collective-permute-start.5 = (bf16[4,1040,128]{2,1,0:T(8,128)(2,1)S(1)}, bf16[4,1040,128]{2,1,0:T(8,128)(2,1)S(1)}, u32[]{:S(2)}, u32[]{:S(2)}) collective-permute-start(bf16[4,1040,128]{2,1,0:T(8,128)(2,1)S(1)} %gate.8), channel_id=1, source_target_pairs={{0,12},{1,13},{2,14},{3,15},{4,0},{5,1},{6,2},{7,3},{8,4},{9,5},{1... | collective-permute-start | bytes 3194888 | tf_op jit(solution)/shard_map/tiles_over_z/ppermute | solution.py:33
  42.0 23.3 %collective-permute-start.6 = (bf16[4,1040,128]{2,1,0:T(8,128)(2,1)S(1)}, bf16[4,1040,128]{2,1,0:T(8,128)(2,1)S(1)}, u32[]{:S(2)}, u32[]{:S(2)}) collective-permute-start(bf16[4,1040,128]{2,1,0:T(8,128)(2,1)S(1)} %gate.7.refs_2_), channel_id=1, source_target_pairs={{0,4},{1,5},{2,6},{3,7},{4,8},{5,9},{6,10},{7,11},{8,12},{9,13},{1... | collective-permute-start | bytes 3194888 | tf_op jit(solution)/shard_map/tiles_over_z/ppermute | solution.py:33
  42.0 30.2 %collective-permute-start.7 = (bf16[193,16,128]{2,1,0:T(8,128)(2,1)S(1)}, bf16[193,16,128]{2,1,0:T(8,128)(2,1)S(1)}, u32[]{:S(2)}, u32[]{:S(2)}) collective-permute-start(bf16[193,16,128]{2,1,0:T(8,128)(2,1)S(1)} %get-tuple-element.67), channel_id=1, source_target_pairs={{0,1},{1,2},{2,3},{3,0},{4,5},{5,6},{6,7},{7,4},{8,9},{9,10},{10,1... | collective-permute-start | bytes 2371592 | tf_op jit(solution)/shard_map/tiles_over_y/ppermute | solution.py:33
  42.0 30.2 %collective-permute-start.8 = (bf16[193,16,128]{2,1,0:T(8,128)(2,1)S(1)}, bf16[193,16,128]{2,1,0:T(8,128)(2,1)S(1)}, u32[]{:S(2)}, u32[]{:S(2)}) collective-permute-start(bf16[193,16,128]{2,1,0:T(8,128)(2,1)S(1)} %get-tuple-element.66), channel_id=1, source_target_pairs={{0,2},{1,3},{2,0},{3,1},{4,6},{5,7},{6,4},{7,5},{8,10},{9,11},{10,... | collective-permute-start | bytes 2371592 | tf_op jit(solution)/shard_map/tiles_over_y/ppermute | solution.py:33
  73.3 16.3 %collective-permute-start.9 = (bf16[4,1040,128]{2,1,0:T(8,128)(2,1)S(1)}, bf16[4,1040,128]{2,1,0:T(8,128)(2,1)}, u32[]{:S(2)}, u32[]{:S(2)}) collective-permute-start(bf16[4,1040,128]{2,1,0:T(8,128)(2,1)S(1)} %stack.57.refs_0_.refs_1_), channel_id=1, source_target_pairs={{0,4},{1,5},{2,6},{3,7},{4,8},{5,9},{6,10},{7,11},{8,12},{9,13},{1... | collective-permute-start | bytes 3194888 | tf_op jit(solution)/shard_map/tiles_over_z/ppermute | solution.py:33
  91.1 4.2 %collective-permute-start.10 = (bf16[4,4,2,128,256]{4,3,2,1,0:T(8,128)(2,1)S(1)}, bf16[4,4,2,128,256]{4,3,2,1,0:T(8,128)(2,1)S(1)}, u32[]{:S(2)}, u32[]{:S(2)}) collective-permute-start(bf16[4,4,2,128,256]{4,3,2,1,0:T(8,128)(2,1)S(1)} %gate.10), channel_id=1, source_target_pairs={{0,16},{16,0},{32,48},{48,32},{64,80},{80,64},{96,112},{112,96},{1... | collective-permute-start | bytes 6291464 | tf_op jit(solution)/shard_map/sum_cores/ppermute | solution.py:37
  91.3 27.2 %copy-start.6 = (bf16[193,16,128]{2,1,0:T(8,128)(2,1)S(1)}, bf16[193,16,128]{2,1,0:T(8,128)(2,1)}, u32[]{:S(2)}) copy-start(bf16[193,16,128]{2,1,0:T(8,128)(2,1)} %copy-done.4) | copy-start | bytes 2371588
  91.3 27.2 %copy-start.9 = (bf16[193,16,128]{2,1,0:T(8,128)(2,1)S(1)}, bf16[193,16,128]{2,1,0:T(8,128)(2,1)}, u32[]{:S(2)}) copy-start(bf16[193,16,128]{2,1,0:T(8,128)(2,1)} %copy-done.7) | copy-start | bytes 2371588
  91.3 26.2 %collective-permute-start.17 = (bf16[4,1040,128]{2,1,0:T(8,128)(2,1)S(1)}, bf16[4,1040,128]{2,1,0:T(8,128)(2,1)S(1)}, u32[]{:S(2)}, u32[]{:S(2)}) collective-permute-start(bf16[4,1040,128]{2,1,0:T(8,128)(2,1)S(1)} %gate.11), channel_id=1, source_target_pairs={{0,12},{1,13},{2,14},{3,15},{4,0},{5,1},{6,2},{7,3},{8,4},{9,5},{1... | collective-permute-start | bytes 3194888 | tf_op jit(solution)/shard_map/tiles_over_z/ppermute | solution.py:33
  92.3 26.2 %collective-permute-start.18 = (bf16[4,1040,128]{2,1,0:T(8,128)(2,1)S(1)}, bf16[4,1040,128]{2,1,0:T(8,128)(2,1)S(1)}, u32[]{:S(2)}, u32[]{:S(2)}) collective-permute-start(bf16[4,1040,128]{2,1,0:T(8,128)(2,1)S(1)} %gate.9.refs_2_), channel_id=1, source_target_pairs={{0,4},{1,5},{2,6},{3,7},{4,8},{5,9},{6,10},{7,11},{8,12},{9,13},{1... | collective-permute-start | bytes 3194888 | tf_op jit(solution)/shard_map/tiles_over_z/ppermute | solution.py:33
  95.7 13.9 %collective-permute-start.11 = (bf16[4,2,128,256]{3,2,1,0:T(8,128)(2,1)S(1)}, bf16[4,2,128,256]{3,2,1,0:T(8,128)(2,1)S(1)}, u32[]{:S(2)}, u32[]{:S(2)}) collective-permute-start(bf16[4,2,128,256]{3,2,1,0:T(8,128)(2,1)S(1)} %get-tuple-element.36), channel_id=1, source_target_pairs={{0,32},{1,33},{2,34},{3,35},{4,36},{5,37},{6,38},{7,39},{8,40},{9,... | collective-permute-start | bytes 1572872 | tf_op jit(solution)/shard_map/sum_x/ppermute | solution.py:33
  96.2 16.5 %collective-permute-start.12 = (bf16[4,2,128,256]{3,2,1,0:T(8,128)(2,1)S(1)}, bf16[4,2,128,256]{3,2,1,0:T(8,128)(2,1)S(1)}, u32[]{:S(2)}, u32[]{:S(2)}) collective-permute-start(bf16[4,2,128,256]{3,2,1,0:T(8,128)(2,1)S(1)} %get-tuple-element.37), channel_id=1, source_target_pairs={{0,64},{1,65},{2,66},{3,67},{4,68},{5,69},{6,70},{7,71},{8,72},{9,... | collective-permute-start | bytes 1572872 | tf_op jit(solution)/shard_map/sum_x/ppermute | solution.py:33
  125.0 4.2 %collective-permute-start.19 = (bf16[4,4,2,128,256]{4,3,2,1,0:T(8,128)(2,1)S(1)}, bf16[4,4,2,128,256]{4,3,2,1,0:T(8,128)(2,1)S(1)}, u32[]{:S(2)}, u32[]{:S(2)}) collective-permute-start(bf16[4,4,2,128,256]{4,3,2,1,0:T(8,128)(2,1)S(1)} %get-tuple-element.44), channel_id=1, source_target_pairs={{0,16},{16,0},{32,48},{48,32},{64,80},{80,64},{96,112},{112,96},{1... | collective-permute-start | bytes 6291464 | tf_op jit(solution)/shard_map/sum_cores/ppermute | solution.py:37
  125.1 13.6 %collective-permute-start.13 = (bf16[4,2,128,256]{3,2,1,0:T(8,128)(2,1)S(1)}, bf16[4,2,128,256]{3,2,1,0:T(8,128)(2,1)S(1)}, u32[]{:S(2)}, u32[]{:S(2)}) collective-permute-start(bf16[4,2,128,256]{3,2,1,0:T(8,128)(2,1)S(1)} %get-tuple-element.38), channel_id=1, source_target_pairs={{0,96},{1,97},{2,98},{3,99},{4,100},{5,101},{6,102},{7,103},{8,104... | collective-permute-start | bytes 1572872 | tf_op jit(solution)/shard_map/sum_x/ppermute | solution.py:33
  129.6 20.4 %collective-permute-start.20 = (bf16[4,2,128,256]{3,2,1,0:T(8,128)(2,1)S(1)}, bf16[4,2,128,256]{3,2,1,0:T(8,128)(2,1)S(1)}, u32[]{:S(2)}, u32[]{:S(2)}) collective-permute-start(bf16[4,2,128,256]{3,2,1,0:T(8,128)(2,1)S(1)} %get-tuple-element.45), channel_id=1, source_target_pairs={{0,32},{1,33},{2,34},{3,35},{4,36},{5,37},{6,38},{7,39},{8,40},{9,... | collective-permute-start | bytes 1572872 | tf_op jit(solution)/shard_map/sum_x/ppermute | solution.py:33
  130.2 19.9 %collective-permute-start.21 = (bf16[4,2,128,256]{3,2,1,0:T(8,128)(2,1)S(1)}, bf16[4,2,128,256]{3,2,1,0:T(8,128)(2,1)S(1)}, u32[]{:S(2)}, u32[]{:S(2)}) collective-permute-start(bf16[4,2,128,256]{3,2,1,0:T(8,128)(2,1)S(1)} %get-tuple-element.46), channel_id=1, source_target_pairs={{0,64},{1,65},{2,66},{3,67},{4,68},{5,69},{6,70},{7,71},{8,72},{9,... | collective-permute-start | bytes 1572872 | tf_op jit(solution)/shard_map/sum_x/ppermute | solution.py:33
  132.6 25.5 %collective-permute-start.22 = (bf16[4,2,128,256]{3,2,1,0:T(8,128)(2,1)S(1)}, bf16[4,2,128,256]{3,2,1,0:T(8,128)(2,1)S(1)}, u32[]{:S(2)}, u32[]{:S(2)}) collective-permute-start(bf16[4,2,128,256]{3,2,1,0:T(8,128)(2,1)S(1)} %get-tuple-element.47), channel_id=1, source_target_pairs={{0,96},{1,97},{2,98},{3,99},{4,100},{5,101},{6,102},{7,103},{8,104... | collective-permute-start | bytes 1572872 | tf_op jit(solution)/shard_map/sum_x/ppermute | solution.py:33
  139.1 19.3 %collective-permute-start.14 = (bf16[2,128,256]{2,1,0:T(8,128)(2,1)S(1)}, bf16[2,128,256]{2,1,0:T(8,128)(2,1)S(1)}, u32[]{:S(2)}, u32[]{:S(2)}) collective-permute-start(bf16[2,128,256]{2,1,0:T(8,128)(2,1)S(1)} %get-tuple-element.40), channel_id=1, source_target_pairs={{0,3},{1,0},{2,1},{3,2},{4,7},{5,4},{6,5},{7,6},{8,11},{9,8},{10,9... | collective-permute-start | bytes 393224 | tf_op jit(solution)/shard_map/coeffs_over_y/ppermute | solution.py:33
  139.2 19.3 %collective-permute-start.15 = (bf16[2,128,256]{2,1,0:T(8,128)(2,1)S(1)}, bf16[2,128,256]{2,1,0:T(8,128)(2,1)S(1)}, u32[]{:S(2)}, u32[]{:S(2)}) collective-permute-start(bf16[2,128,256]{2,1,0:T(8,128)(2,1)S(1)} %get-tuple-element.41), channel_id=1, source_target_pairs={{0,2},{1,3},{2,0},{3,1},{4,6},{5,7},{6,4},{7,5},{8,10},{9,11},{10,... | collective-permute-start | bytes 393224 | tf_op jit(solution)/shard_map/coeffs_over_y/ppermute | solution.py:33
  150.0 8.4 %copy-start.12 = (f32[2,64,64]{2,1,0:T(8,128)S(1)}, f32[2,64,64]{2,1,0:T(8,128)}, u32[]{:S(2)}) copy-start(f32[2,64,64]{2,1,0:T(8,128)} %refs_5_.7) | copy-start | bytes 98308
  150.0 8.4 %collective-permute-start.16 = (bf16[2,128,256]{2,1,0:T(8,128)(2,1)S(1)}, bf16[2,128,256]{2,1,0:T(8,128)(2,1)S(1)}, u32[]{:S(2)}, u32[]{:S(2)}) collective-permute-start(bf16[2,128,256]{2,1,0:T(8,128)(2,1)S(1)} %get-tuple-element.42), channel_id=1, source_target_pairs={{0,1},{1,2},{2,3},{3,0},{4,5},{5,6},{6,7},{7,4},{8,9},{9,10},{10,1... | collective-permute-start | bytes 393224 | tf_op jit(solution)/shard_map/coeffs_over_y/ppermute | solution.py:33
  159.4 7.9 %collective-permute-start.26 = (bf16[2,2,16,2048]{3,2,1,0:T(8,128)(2,1)S(1)}, bf16[2,2,16,2048]{3,2,1,0:T(8,128)(2,1)S(1)}, u32[]{:S(2)}, u32[]{:S(2)}) collective-permute-start(bf16[2,2,16,2048]{3,2,1,0:T(8,128)(2,1)S(1)} %get-tuple-element.53), channel_id=1, source_target_pairs={{0,32},{1,33},{2,34},{3,35},{4,36},{5,37},{6,38},{7,39},{8,40},{9,... | collective-permute-start | bytes 786440 | tf_op jit(solution)/shard_map/exchange_over_row/ppermute | solution.py:33
  161.4 13.9 %collective-permute-start.23 = (bf16[2,128,256]{2,1,0:T(8,128)(2,1)S(1)}, bf16[2,128,256]{2,1,0:T(8,128)(2,1)S(1)}, u32[]{:S(2)}, u32[]{:S(2)}) collective-permute-start(bf16[2,128,256]{2,1,0:T(8,128)(2,1)S(1)} %get-tuple-element.50), channel_id=1, source_target_pairs={{0,3},{1,0},{2,1},{3,2},{4,7},{5,4},{6,5},{7,6},{8,11},{9,8},{10,9... | collective-permute-start | bytes 393224 | tf_op jit(solution)/shard_map/coeffs_over_y/ppermute | solution.py:33
  161.4 13.9 %collective-permute-start.24 = (bf16[2,128,256]{2,1,0:T(8,128)(2,1)S(1)}, bf16[2,128,256]{2,1,0:T(8,128)(2,1)S(1)}, u32[]{:S(2)}, u32[]{:S(2)}) collective-permute-start(bf16[2,128,256]{2,1,0:T(8,128)(2,1)S(1)} %get-tuple-element.51), channel_id=1, source_target_pairs={{0,2},{1,3},{2,0},{3,1},{4,6},{5,7},{6,4},{7,5},{8,10},{9,11},{10,... | collective-permute-start | bytes 393224 | tf_op jit(solution)/shard_map/coeffs_over_y/ppermute | solution.py:33
  162.3 13.1 %collective-permute-start.25 = (bf16[2,128,256]{2,1,0:T(8,128)(2,1)S(1)}, bf16[2,128,256]{2,1,0:T(8,128)(2,1)S(1)}, u32[]{:S(2)}, u32[]{:S(2)}) collective-permute-start(bf16[2,128,256]{2,1,0:T(8,128)(2,1)S(1)} %get-tuple-element.52), channel_id=1, source_target_pairs={{0,1},{1,2},{2,3},{3,0},{4,5},{5,6},{6,7},{7,4},{8,9},{9,10},{10,1... | collective-permute-start | bytes 393224 | tf_op jit(solution)/shard_map/coeffs_over_y/ppermute | solution.py:33
  163.4 11.8 %collective-permute-start.27 = (bf16[2,2,16,2048]{3,2,1,0:T(8,128)(2,1)S(1)}, bf16[2,2,16,2048]{3,2,1,0:T(8,128)(2,1)S(1)}, u32[]{:S(2)}, u32[]{:S(2)}) collective-permute-start(bf16[2,2,16,2048]{3,2,1,0:T(8,128)(2,1)S(1)} %get-tuple-element.54), channel_id=1, source_target_pairs={{0,64},{1,65},{2,66},{3,67},{4,68},{5,69},{6,70},{7,71},{8,72},{9,... | collective-permute-start | bytes 786440 | tf_op jit(solution)/shard_map/exchange_over_row/ppermute | solution.py:33
  167.2 14.4 %collective-permute-start.28 = (bf16[2,2,16,2048]{3,2,1,0:T(8,128)(2,1)S(1)}, bf16[2,2,16,2048]{3,2,1,0:T(8,128)(2,1)S(1)}, u32[]{:S(2)}, u32[]{:S(2)}) collective-permute-start(bf16[2,2,16,2048]{3,2,1,0:T(8,128)(2,1)S(1)} %get-tuple-element.57), channel_id=1, source_target_pairs={{0,96},{1,97},{2,98},{3,99},{4,100},{5,101},{6,102},{7,103},{8,104... | collective-permute-start | bytes 786440 | tf_op jit(solution)/shard_map/exchange_over_row/ppermute | solution.py:33
  176.3 15.0 %collective-permute-start.32 = (bf16[2,2,16,2048]{3,2,1,0:T(8,128)(2,1)S(1)}, bf16[2,2,16,2048]{3,2,1,0:T(8,128)(2,1)S(1)}, u32[]{:S(2)}, u32[]{:S(2)}) collective-permute-start(bf16[2,2,16,2048]{3,2,1,0:T(8,128)(2,1)S(1)} %get-tuple-element.61), channel_id=1, source_target_pairs={{0,96},{1,97},{2,98},{3,99},{4,100},{5,101},{6,102},{7,103},{8,104... | collective-permute-start | bytes 786440 | tf_op jit(solution)/shard_map/exchange_over_row/ppermute | solution.py:33
  176.9 14.5 %collective-permute-start.31 = (bf16[2,2,16,2048]{3,2,1,0:T(8,128)(2,1)S(1)}, bf16[2,2,16,2048]{3,2,1,0:T(8,128)(2,1)S(1)}, u32[]{:S(2)}, u32[]{:S(2)}) collective-permute-start(bf16[2,2,16,2048]{3,2,1,0:T(8,128)(2,1)S(1)} %get-tuple-element.60), channel_id=1, source_target_pairs={{0,64},{1,65},{2,66},{3,67},{4,68},{5,69},{6,70},{7,71},{8,72},{9,... | collective-permute-start | bytes 786440 | tf_op jit(solution)/shard_map/exchange_over_row/ppermute | solution.py:33
  177.2 14.2 %collective-permute-start.30 = (bf16[2,2,16,2048]{3,2,1,0:T(8,128)(2,1)S(1)}, bf16[2,2,16,2048]{3,2,1,0:T(8,128)(2,1)S(1)}, u32[]{:S(2)}, u32[]{:S(2)}) collective-permute-start(bf16[2,2,16,2048]{3,2,1,0:T(8,128)(2,1)S(1)} %get-tuple-element.59), channel_id=1, source_target_pairs={{0,32},{1,33},{2,34},{3,35},{4,36},{5,37},{6,38},{7,39},{8,40},{9,... | collective-permute-start | bytes 786440 | tf_op jit(solution)/shard_map/exchange_over_row/ppermute | solution.py:33
  181.8 9.9 %collective-permute-start.29 = (bf16[4,2,16,2048]{3,2,1,0:T(8,128)(2,1)S(1)}, bf16[4,2,16,2048]{3,2,1,0:T(8,128)(2,1)S(1)}, u32[]{:S(2)}, u32[]{:S(2)}) collective-permute-start(bf16[4,2,16,2048]{3,2,1,0:T(8,128)(2,1)S(1)} %pad_maximum_fusion), channel_id=1, source_target_pairs={{0,16},{16,0},{32,48},{48,32},{64,80},{80,64},{96,112},{112,96},{1... | collective-permute-start | bytes 1572872 | tf_op jit(solution)/shard_map/exchange_over_row/ppermute | solution.py:37
  191.5 2.0 collective-permute-start.33
  195.5 5.2 %collective-permute-start.36 = (f32[32,128]{1,0:T(8,128)S(1)}, f32[32,128]{1,0:T(8,128)S(1)}, u32[]{:S(2)}, u32[]{:S(2)}) collective-permute-start(f32[32,128]{1,0:T(8,128)S(1)} %get-tuple-element.65), channel_id=1, source_target_pairs={{0,96},{1,97},{2,98},{3,99},{4,100},{5,101},{6,102},{7,103},{8,104... | collective-permute-start | bytes 49160 | tf_op jit(solution)/shard_map/exchange/ppermute | solution.py:33
  195.5 5.1 %collective-permute-start.34 = (f32[32,128]{1,0:T(8,128)S(1)}, f32[32,128]{1,0:T(8,128)S(1)}, u32[]{:S(2)}, u32[]{:S(2)}) collective-permute-start(f32[32,128]{1,0:T(8,128)S(1)} %get-tuple-element.63), channel_id=1, source_target_pairs={{0,32},{1,33},{2,34},{3,35},{4,36},{5,37},{6,38},{7,39},{8,40},{9,... | collective-permute-start | bytes 49160 | tf_op jit(solution)/shard_map/exchange/ppermute | solution.py:33
  198.8 5.2 %collective-permute-start.35 = (f32[32,128]{1,0:T(8,128)S(1)}, f32[32,128]{1,0:T(8,128)S(1)}, u32[]{:S(2)}, u32[]{:S(2)}) collective-permute-start(f32[32,128]{1,0:T(8,128)S(1)} %get-tuple-element.64), channel_id=1, source_target_pairs={{0,64},{1,65},{2,66},{3,67},{4,68},{5,69},{6,70},{7,71},{8,72},{9,... | collective-permute-start | bytes 49160 | tf_op jit(solution)/shard_map/exchange/ppermute | solution.py:33
  204.0 1.3 collective-permute-start.37
  205.3 5.2 %collective-permute-start.40 = (f32[2,16,128]{2,1,0:T(8,128)S(1)}, f32[2,16,128]{2,1,0:T(8,128)S(1)}, u32[]{:S(2)}, u32[]{:S(2)}) collective-permute-start(f32[2,16,128]{2,1,0:T(8,128)S(1)} %pad_maximum_fusion.2), channel_id=1, source_target_pairs={{0,3},{1,0},{2,1},{3,2},{4,7},{5,4},{6,5},{7,6},{8,11},{9,8},{10,9... | collective-permute-start | bytes 49160 | tf_op jit(solution)/shard_map/exchange/ppermute | solution.py:33
  206.4 4.9 %collective-permute-start.38 = (f32[2,16,128]{2,1,0:T(8,128)S(1)}, f32[2,16,128]{2,1,0:T(8,128)S(1)}, u32[]{:S(2)}, u32[]{:S(2)}) collective-permute-start(f32[2,16,128]{2,1,0:T(8,128)S(1)} %pad_maximum_fusion.2), channel_id=1, source_target_pairs={{0,1},{1,2},{2,3},{3,0},{4,5},{5,6},{6,7},{7,4},{8,9},{9,10},{10,1... | collective-permute-start | bytes 49160 | tf_op jit(solution)/shard_map/exchange/ppermute | solution.py:33
  207.4 5.2 %collective-permute-start.39 = (f32[2,16,128]{2,1,0:T(8,128)S(1)}, f32[2,16,128]{2,1,0:T(8,128)S(1)}, u32[]{:S(2)}, u32[]{:S(2)}) collective-permute-start(f32[2,16,128]{2,1,0:T(8,128)S(1)} %pad_maximum_fusion.2), channel_id=1, source_target_pairs={{0,2},{1,3},{2,0},{3,1},{4,6},{5,7},{6,4},{7,5},{8,10},{9,11},{10,... | collective-permute-start | bytes 49160 | tf_op jit(solution)/shard_map/exchange/ppermute | solution.py:33
  212.6 7.2 %collective-permute-start.43 = (f32[2,16,128]{2,1,0:T(8,128)S(1)}, f32[2,16,128]{2,1,0:T(8,128)S(1)}, u32[]{:S(2)}, u32[]{:S(2)}) collective-permute-start(f32[2,16,128]{2,1,0:T(8,128)S(1)} %add_add_fusion), channel_id=1, source_target_pairs={{0,12},{1,13},{2,14},{3,15},{4,0},{5,1},{6,2},{7,3},{8,4},{9,5},{1... | collective-permute-start | bytes 49160 | tf_op jit(solution)/shard_map/exchange/ppermute | solution.py:33
  213.1 6.8 %collective-permute-start.41 = (f32[2,16,128]{2,1,0:T(8,128)S(1)}, f32[2,16,128]{2,1,0:T(8,128)S(1)}, u32[]{:S(2)}, u32[]{:S(2)}) collective-permute-start(f32[2,16,128]{2,1,0:T(8,128)S(1)} %add_add_fusion), channel_id=1, source_target_pairs={{0,4},{1,5},{2,6},{3,7},{4,8},{5,9},{6,10},{7,11},{8,12},{9,13},{1... | collective-permute-start | bytes 49160 | tf_op jit(solution)/shard_map/exchange/ppermute | solution.py:33
  214.7 5.2 %collective-permute-start.42 = (f32[2,16,128]{2,1,0:T(8,128)S(1)}, f32[2,16,128]{2,1,0:T(8,128)S(1)}, u32[]{:S(2)}, u32[]{:S(2)}) collective-permute-start(f32[2,16,128]{2,1,0:T(8,128)S(1)} %add_add_fusion), channel_id=1, source_target_pairs={{0,8},{1,9},{2,10},{3,11},{4,12},{5,13},{6,14},{7,15},{8,0},{9,1},... | collective-permute-start | bytes 49160 | tf_op jit(solution)/shard_map/exchange/ppermute | solution.py:33
  (13 other events, 39.3 us)
where the time goes:
time: 221 us
  waiting for transfers between devices  122 us (55%)
  starting transfers between devices  57.5 us (26%)
  Pallas kernels  27.1 us (12%)
  local copies, waits for them, and re-layouts  10.3 us (5%)
  between operations  2.46 us (1%)
    ppermute x39, waiting for transfers between devices, move(): return lax.ppermute(value, ('row', 'col'), pairs)  114 us
    ppermute x39, starting transfers between devices, move(): return lax.ppermute(value, ('row', 'col'), pairs)  57 us
    pallas_call x18, Pallas kernels, call(): pl.pallas_call(kernel, out_shape=out_shape, in_specs=list(in_specs) + [VM...  22.9 us
    unnamed x34, local copies, waits for them, and re-layouts  9.56 us
    ppermute x5, waiting for transfers between devices, swap_core(): return lax.ppermute(value, 'row', [(r, r ^ 1) for r in range(8)])  8.18 us
  transfers between devices with their start and end apart: 44, of which 25 were waited for; matrix products, arithmetic and copies ran while one was open for 0% of the time, Pallas kernels for 6%

commit v1 on v0

--- a/solution.py
+++ b/solution.py
@@ -33,6 +33,11 @@
     return lax.ppermute(value, ("row", "col"), pairs)
 
 
+def trade(value, axis, mask):
+    pairs = [(c, c ^ (mask if axis == "y" else 4 * mask)) for c in range(16)]
+    return lax.ppermute(value, "col", pairs)
+
+
 def swap_core(value):
     return lax.ppermute(value, "row", [(r, r ^ 1) for r in range(8)])
 
@@ -69,7 +74,7 @@
     return call(copy_body, shape, [VMEM], "gate", (value,), after, nbytes=2 * value.size * 2)
 
 
-def relayout_body(parts, yc_ref, x_ref, *refs):
+def relayout_body(parts, spot_ref, x_ref, *refs):
     *orbitals, out, wide = refs
     wide[...] = x_ref[...].reshape(wide.shape).astype(F32)
     row = 0
@@ -78,7 +83,7 @@
             for u in range(16 * r + offset, 16 * r + offset + count):
                 out[0, row] = wide[pl.ds(u, 16, stride=128), :].astype(BF16)
                 row += 1
-        out[0, row] = jnp.full((16, 128), yc_ref[2].astype(F32), F32).astype(BF16)
+        out[0, row] = jnp.full((16, 128), spot_ref[4].astype(F32), F32).astype(BF16)
         row += 1
     for ref in orbitals:
         for half in range(2):
@@ -86,9 +91,9 @@
             row += 64
 
 
-def relayout(tile, yc, parts, orbitals):
-    def block(step, yc_ref):
-        return ((yc_ref[0] + step * yc_ref[1] + 4) % 4, 0, 0)
+def relayout(tile, spot, parts, orbitals):
+    def block(step, spot_ref):
+        return ((spot_ref[3] + step * spot_ref[2] + 4) % 4, 0, 0)
 
     blocks = sum(8 * count + 1 for _, count in parts) + 128 * len(orbitals)
     return pl.pallas_call(
@@ -97,14 +102,14 @@
             num_scalar_prefetch=1,
             grid=(4,),
             in_specs=[pl.BlockSpec((16, 128, 128), block)] + [VMEM] * len(orbitals),
-            out_specs=pl.BlockSpec((1, blocks, 16, 128), lambda step, yc_ref: (step, 0, 0, 0)),
+            out_specs=pl.BlockSpec((1, blocks, 16, 128), lambda step, spot_ref: (step, 0, 0, 0)),
             scratch_shapes=[pltpu.VMEM((2048, 128), F32)],
         ),
         out_shape=jax.ShapeDtypeStruct((4, blocks, 16, 128), BF16),
         name="relayout",
         compiler_params=pltpu.CompilerParams(vmem_limit_bytes=8 * 1024 * 1024),
         cost_estimate=pl.CostEstimate(flops=0, bytes_accessed=4 << 20, transcendentals=0),
-    )(yc, tile, *orbitals)
+    )(spot, tile, *orbitals)
 
 
 def stack_body(start, first, a, b, c, out):
@@ -114,66 +119,64 @@
         out[i + 1] = ref[start:start + blocks].reshape(out.shape[1:])
 
 
-def product_body(count, xky_ref, t0, t1, t2, t3, orb, o1, o2, o3, own, peer, rows, orbs):
+def product_body(count, h, spot_ref, t0, t1, t2, t3, orb, o1, o2, o3, out, rows, orbs):
     rp = 16 * count
-    x, k, sign = xky_ref[0], xky_ref[1], xky_ref[2]
+    x, k, sign = spot_ref[0], spot_ref[1], spot_ref[2]
     for ref in (t0, t1, t2, t3):
         for i in range(4):
             code = jnp.max(ref[i, 8 * rp:8 * rp + 16, :].astype(F32)).astype(jnp.int32)
             m = code >> 3
             lane = pl.multiple_of((code & 7) * 128, 128)
-            for h in range(2):
-                for e in range(4):
-                    towards = (x + sign * e + 4) % 4 if h == 0 else (x - sign * e + 4) % 4
-                    source = pl.multiple_of((((k + h) % 2) * 4 + towards) * rp, rp)
-                    place = (h * 4 + e) * rp
-                    rows[m, place:place + rp, pl.ds(lane, 128)] = ref[i, pl.ds(source, rp), :]
+            for e in range(4):
+                towards = (x + sign * e + 4) % 4 if h == 0 else (x - sign * e + 4) % 4
+                source = pl.multiple_of((((k + h) % 2) * 4 + towards) * rp, rp)
+                rows[m, e * rp:(e + 1) * rp, pl.ds(lane, 128)] = ref[i, pl.ds(source, rp), :]
     orbs[0] = orb[...]
     for d, ref in enumerate((o1, o2, o3)):
         for half in range(2):
             start = ref.shape[0] - 128 + 64 * half
             orbs[d + 1, :, half * 128:(half + 1) * 128] = ref[start:start + 64].reshape(1024, 128)
-    for h, out in ((1, peer), (0, own)):
-        for d in range(4):
-            orb = orbs[d]
-            place = d if h == 0 else (4 - d) % 4
-            for m in range(2):
-                acc = jnp.dot(rows[m, h * 4 * rp:(h + 1) * 4 * rp, :], orb, preferred_element_type=F32)
-                for e in range(4):
-                    out[e, place, m] = acc[e * rp:(e + 1) * rp].astype(BF16)
-
-
-def product(count, xky, tiles, orbs, after):
+    for d in range(4):
+        place = d if h == 0 else (4 - d) % 4
+        for m in range(2):
+            acc = jnp.dot(rows[m], orbs[d], preferred_element_type=F32)
+            for e in range(4):
+                out[e, place, m] = acc[e * rp:(e + 1) * rp].astype(BF16)
+
+
+def product(count, h, spot, tiles, orbs, after):
     rp = 16 * count
-    shape = jax.ShapeDtypeStruct((4, 4, 2, rp, 256), BF16)
     return call(
-        functools.partial(product_body, count),
-        [shape, shape],
+        functools.partial(product_body, count, h),
+        jax.ShapeDtypeStruct((4, 4, 2, rp, 256), BF16),
         [SMEM] + [VMEM] * 8,
         "product",
-        (xky, *tiles, *orbs),
+        (spot, *tiles, *orbs),
         after,
-        scratch=[pltpu.VMEM((2, 8 * rp, 1024), BF16), pltpu.VMEM((4, 1024, 256), BF16)],
-        flops=2 * 2 * 8 * rp * 1024 * 1024,
+        scratch=[pltpu.VMEM((2, 4 * rp, 1024), BF16), pltpu.VMEM((4, 1024, 256), BF16)],
+        flops=2 * 2 * 4 * rp * 1024 * 1024,
         nbytes=6 << 20,
         limit=14,
     )
 
 
-def pair_body(a, b, *outs):
-    for e, out in enumerate(outs):
-        out[...] = (a[e + 1].astype(F32) + b[e + 1].astype(F32)).astype(BF16)
-
-
-def total_body(a, b, j1, j2, j3, *outs):
+def pair_body(a, b, ahead, behind):
+    ahead[...] = (a[2].astype(F32) + b[2].astype(F32)).astype(BF16)
+    behind[...] = (a[3].astype(F32) + b[3].astype(F32)).astype(BF16)
+
+
+def relay_body(a, b, passing, out):
+    out[...] = (a[1].astype(F32) + b[1].astype(F32) + passing[...].astype(F32)).astype(BF16)
+
+
+def total_body(a, b, j1, j2, *outs):
     for d, out in enumerate(outs):
         value = a[0, d].astype(F32) + b[0, d].astype(F32)
-        value = value + j1[d].astype(F32) + j2[d].astype(F32) + j3[d].astype(F32)
-        out[...] = value.astype(BF16)
-
-
-def fit_body(count, xky_ref, c0, c1, c2, c3, metric, fitted, s0, s1, s2, s3, coef, fit):
-    x, k, sign, y = xky_ref[0], xky_ref[1], xky_ref[2], xky_ref[3]
+        out[...] = (value + j1[d].astype(F32) + j2[d].astype(F32)).astype(BF16)
+
+
+def fit_body(count, spot_ref, c0, c1, c2, c3, metric, fitted, s0, s1, s2, s3, coef, fit):
+    x, k, sign, y = spot_ref[0], spot_ref[1], spot_ref[2], spot_ref[3]
     for d, ref in enumerate((c0, c1, c2, c3)):
         row = pl.multiple_of(((y + sign * d + 4) % 4) * 16, 16)
         for m in range(2):
@@ -194,7 +197,7 @@
             out[h, 1] = coef[m, pl.ds(q, 16), :]
 
 
-def fit_part(count, xky, pieces, metric, after):
+def fit_part(count, spot, pieces, metric, after):
     lanes = 256 * count
     shape = jax.ShapeDtypeStruct((2, 64, lanes), BF16)
     send = jax.ShapeDtypeStruct((2, 2, 16, lanes), BF16)
@@ -203,7 +206,7 @@
         [shape, send, send, send, send],
         [SMEM] + [VMEM] * 5,
         "fit",
-        (xky, *pieces, metric),
+        (spot, *pieces, metric),
         after,
         scratch=[pltpu.VMEM((2, 64, lanes), BF16), pltpu.VMEM((2, 64, lanes), BF16)],
         flops=2 * 2 * 64 * 128 * lanes,
@@ -219,14 +222,13 @@
                 out[m, :, offset + uu, :] = ref[m, :, uu * 256:(uu + 1) * 256]
 
 
-def exchange_body(parts, xk_ref, *refs):
+def exchange_body(parts, spot_ref, *refs):
     *outs, total = refs[-9:-4]
     wides = refs[-4:]
-    x, k, sign = xk_ref[0], xk_ref[1], xk_ref[2]
+    x, k, sign = spot_ref[0], spot_ref[1], spot_ref[2]
     refs = refs[:-9]
     for part, (offset, count) in enumerate(parts):
-        near = refs[5 * part:5 * part + 4]
-        far = refs[5 * part + 4]
+        near, far = refs[4 * part:4 * part + 4], refs[-1]
         for e in range(4):
             for h in range(2):
                 source = (x - sign * e + 4) % 4 if h == 0 else (x + sign * e + 4) % 4
@@ -235,8 +237,8 @@
                     row = pl.multiple_of((16 * r + offset + uu) * 16, 16)
                     for index, wide in enumerate(wides):
                         which, lane = index // 2, uu * 256 + index % 2 * 128
-                        lanes = slice(lane, lane + 128)
-                        value = near[e][0, which, :, lanes] if h == 0 else far[e, which, :, lanes]
+                        lanes, far_lanes = (slice(at, at + 128) for at in (lane, offset * 256 + lane))
+                        value = near[e][0, which, :, lanes] if h == 0 else far[e, which, :, far_lanes]
                         wide[pl.ds(row, 16), :] = value.astype(F32)
     acc = jnp.zeros((128, 128), F32)
     for q in range(16):
@@ -254,9 +256,7 @@
     col = lax.axis_index("col").astype(jnp.int32)
     x, k, y = row // 2, row % 2, col % 4
     sign = 1 - 2 * k
-    xk = jnp.stack([x, k, sign])
-    xky = jnp.stack([x, k, sign, y])
-    yc = jnp.stack([y, sign, tile_mu[0] * 8 + tile_nu[0]])
+    spot = jnp.stack([x, k, sign, y, tile_mu[0] * 8 + tile_nu[0]])
     last = len(CHUNKS) - 1
     offsets = [sum(CHUNKS[:i]) for i in range(len(CHUNKS))]
     parts = list(zip(offsets, CHUNKS))
@@ -282,37 +282,38 @@
             across = move(gate(shards[i], [near]), "z", 3)
             gathered[i] = (shards[i], near, across, move(near, "z", 1))
 
-    partial, got, blocks, arrived, pieces = {}, {}, {}, {}, {}
+    partial, got, blocks, arrived = {}, {}, {}, {}
 
     def multiply(i, after):
         with jax.named_scope("products"):
-            partial[i] = product(CHUNKS[i], xky, gathered[i], orbs, after)
+            others = product(CHUNKS[i], 1, spot, gathered[i], orbs, after)
+            partial[i] = (product(CHUNKS[i], 0, spot, gathered[i], orbs, [others]), others)
 
     def sum_rows(i, after):
         mine, others = partial[i]
-        others = gate(others, after) if after else others
         with jax.named_scope("sum_cores"):
             twin = swap_core(others)
             shape = jax.ShapeDtypeStruct(mine.shape[1:], BF16)
-            sends = call(pair_body, [shape] * 3, [VMEM] * 2, "pair", (mine, twin), nbytes=3 << 20)
+            ahead, behind = call(pair_body, [shape] * 2, [VMEM] * 2, "pair", (mine, twin), after, nbytes=3 << 20)
         with jax.named_scope("sum_x"):
-            got[i] = (mine, twin, *[move(send, "x", e + 1) for e, send in enumerate(sends)])
+            passing, behind = move(ahead, "x", 1), move(behind, "x", 3)
+            ahead = call(relay_body, shape, [VMEM] * 3, "relay", (mine, twin, passing), nbytes=2 << 20)
+            got[i] = (mine, twin, behind, move(ahead, "x", 1))
 
     def coeffs(i):
         with jax.named_scope("sum_x"):
             shape = jax.ShapeDtypeStruct(got[i][0].shape[2:], BF16)
-            blocks[i] = call(total_body, [shape] * 4, [VMEM] * 5, "total", got[i], nbytes=2 << 20)
+            blocks[i] = call(total_body, [shape] * 4, [VMEM] * 4, "total", got[i], nbytes=2 << 20)
         with jax.named_scope("coeffs_over_y"):
             blocks[i] = [blocks[i][0]] + [move(blocks[i][d], "y", -d) for d in (1, 2, 3)]
 
     def fit(i, after):
         with jax.named_scope("fit"):
-            fits[i], *sends = fit_part(CHUNKS[i], xky, blocks[i], metric_inverse, after)
+            fits[i], *sends = fit_part(CHUNKS[i], spot, blocks[i], metric_inverse, after)
         with jax.named_scope("exchange_over_row"):
             arrived[i] = [sends[0]] + [move(sends[e], "x", e) for e in (1, 2, 3)]
-            pieces[i] = arrived[i] + [swap_core(jnp.stack([part[1] for part in arrived[i]]))]
-
-    laid = [relayout(tiles[0], yc, group, held) for group, held in zip(groups, ([], [orbitals]))]
+
+    laid = [relayout(tiles[0], spot, group, held) for group, held in zip(groups, ([], [orbitals]))]
     over_y(groups[0], laid[0])
     stack(0, [laid[1]])
     over_y(groups[1], gate(laid[1], [shards[0]]))
@@ -321,7 +322,7 @@
     for i in range(last + 1):
         if i < last:
             stack(i + 1, gathered[i][2:])
-        multiply(i, ([shards[i + 1]] if i < last else []) + (list(got[i - 1][2:4]) if i > 0 else []))
+        multiply(i, ([shards[i + 1]] if i < last else []) + (list(got[i - 1][2:]) if i > 0 else []))
         if i < last:
             gather_z(i + 1, [partial[i][0]])
         sum_rows(i, [gathered[i + 1][1]] if i < last else [])
@@ -343,13 +344,15 @@
         )
 
     with jax.named_scope("exchange"):
-        pieces = [piece for i in range(last + 1) for piece in pieces[i]]
+        far = [jnp.stack([part[1] for part in arrived[i]]) for i in range(last + 1)]
+        far = swap_core(jnp.concatenate(far, axis=3))
+        pieces = [piece for i in range(last + 1) for piece in arrived[i]] + [far]
         blocks = call(
             functools.partial(exchange_body, parts),
             [jax.ShapeDtypeStruct((32, 128), F32)] * 4,
             [SMEM] + [VMEM] * len(pieces),
             "exchange",
-            (xk, *pieces),
+            (spot, *pieces),
             scratch=[pltpu.VMEM((128, 128), F32)] + [pltpu.VMEM((2048, 128), F32)] * 4,
             flops=2 * 128 * 128 * 4096,
             nbytes=2 << 20,
@@ -358,8 +361,8 @@
         keep = jnp.where(k == 0, total[:16], total[16:])
         got = swap_core(jnp.where(k == 0, total[16:], total[:16]))
         total = jnp.stack([jnp.where(k == 0, keep, got), jnp.where(k == 0, got, keep)])
-        for axis in ("y", "z"):
-            total = total + (move(total, axis, 1) + move(total, axis, 2) + move(total, axis, 3))
+        for axis, mask in (("y", 1), ("y", 2), ("z", 1), ("z", 2)):
+            total = total + trade(total, axis, mask)
         exchange = total / 262144.0
     return fitted, exchange
 

time: 221 us -> 219 us (level)
  waiting for transfers between devices: 122 us -> 138 us
  starting transfers between devices: 57.5 us -> 47.8 us
  local copies, waits for them, and re-layouts: 10.3 us -> 2.4 us
    ppermute x39 -> x33, starting transfers between devices: 57 us -> 43 us  [move(): return lax.ppermute(value, ('row', 'col'), pairs)]
    ppermute x0 -> x4, waiting for transfers between devices: none -> 11.1 us  [trade(): return lax.ppermute(value, 'col', pairs)]
    ppermute x39 -> x33, waiting for transfers between devices: 114 us -> 122 us  [move(): return lax.ppermute(value, ('row', 'col'), pairs)]
    unnamed x34 -> x8, local copies, waits for them, and re-layouts: 9.56 us -> 1.6 us
    ppermute x0 -> x4, starting transfers between devices: none -> 4.47 us  [trade(): return lax.ppermute(value, 'col', pairs)]
    ppermute x5 -> x4, waiting for transfers between devices: 8.18 us -> 4.18 us  [swap_core(): return lax.ppermute(value, 'row', [(r, r ^ 1) for r in range(8)])]
    pallas_call x18 -> x21, Pallas kernels: 22.9 us -> 23.4 us  [call(): pl.pallas_call(kernel, out_shape=out_shape, in_specs=list(in_specs) + [VM...]
  transfers between devices with their start and end apart: 44 -> 41, of which waited for: 25 -> 28; matrix products, arithmetic and copies ran while one was open for 0% -> 0% of each run, Pallas kernels for 6% -> 7%
where the time goes in v1:
time: 219 us
  waiting for transfers between devices  138 us (63%)
  starting transfers between devices  47.8 us (22%)
  Pallas kernels  27.7 us (13%)
  between operations  2.43 us (1%)
  local copies, waits for them, and re-layouts  2.4 us (1%)
    ppermute x33, waiting for transfers between devices, move(): return lax.ppermute(value, ('row', 'col'), pairs)  122 us
    ppermute x33, starting transfers between devices, move(): return lax.ppermute(value, ('row', 'col'), pairs)  43 us
    pallas_call x21, Pallas kernels, call(): pl.pallas_call(kernel, out_shape=out_shape, in_specs=list(in_specs) + [VM...  23.4 us
    ppermute x4, waiting for transfers between devices, trade(): return lax.ppermute(value, 'col', pairs)  11.1 us
    ppermute x4, starting transfers between devices, trade(): return lax.ppermute(value, 'col', pairs)  4.47 us
  transfers between devices with their start and end apart: 41, of which 28 were waited for; matrix products, arithmetic and copies ran while one was open for 0% of the time, Pallas kernels for 7%

profile of v1, /device:TPU:6, one launch (start us, length us, event | category | flops | bytes accessed | tf_op | source)
XLA Modules:
  0.0 218.6 jit_solution(14357589423513109353)
XLA Ops:
  2.0 1.6 copy-done.1
  3.6 1.9 relayout.2.refs_0_
  5.7 1.6 collective-permute-start
  7.4 2.9 %collective-permute-start.1 = (bf16[65,16,128]{2,1,0:T(8,128)(2,1)S(1)}, bf16[65,16,128]{2,1,0:T(8,128)(2,1)S(1)}, u32[]{:S(2)}, u32[]{:S(2)}) collective-permute-start(bf16[65,16,128]{2,1,0:T(8,128)(2,1)S(1)} %get-tuple-element.58), channel_id=1, source_target_pairs={{0,2},{1,3},{2,0},{3,1},{4,6},{5,7},{6,4},{7,5},{8,10},{9,11},{10,... | collective-permute-start | bytes 798728 | tf_op jit(solution)/shard_map/tiles_over_y/ppermute | solution.py:33
  11.6 2.3 %relayout.3.refs_0_ = bf16[4,193,16,128]{3,2,1,0:T(8,128)(2,1)S(1)} custom-call(s32[5]{0:T(128)S(1)} %stack.37.spot_ref.refs_0_, bf16[64,128,128]{2,1,0:T(8,128)(2,1)S(1)} %bitcast.54, bf16[1024,256]{1,0:T(8,128)(2,1)S(1)} %copy-done), custom_call_target="tpu_custom_call" | custom-call | bytes 4194304 | tf_op jit(solution)/shard_map/relayout/pallas_call | solution.py:99
  13.9 2.2 collective-permute-done.refs_1_
  16.1 6.5 %collective-permute-done.1.refs_2_ = bf16[65,16,128]{2,1,0:T(8,128)(2,1)S(1)} collective-permute-done((bf16[65,16,128]{2,1,0:T(8,128)(2,1)S(1)}, bf16[65,16,128]{2,1,0:T(8,128)(2,1)S(1)}, u32[]{:S(2)}, u32[]{:S(2)}) %collective-permute-start.1) | collective-permute-done | bytes 266272 | tf_op jit(solution)/shard_map/tiles_over_y/ppermute | solution.py:33
  22.7 2.0 collective-permute-start.3
  26.6 10.8 %collective-permute-done.4.refs_3_.refs_8_ = bf16[193,16,128]{2,1,0:T(8,128)(2,1)S(1)} collective-permute-done((bf16[193,16,128]{2,1,0:T(8,128)(2,1)S(1)}, bf16[193,16,128]{2,1,0:T(8,128)(2,1)S(1)}, u32[]{:S(2)}, u32[]{:S(2)}) %collective-permute-start.4) | collective-permute-done | bytes 790560 | tf_op jit(solution)/shard_map/tiles_over_y/ppermute | solution.py:33
  37.4 2.3 %collective-permute-done.3.refs_0_ = bf16[4,1040,128]{2,1,0:T(8,128)(2,1)S(1)} collective-permute-done((bf16[4,1040,128]{2,1,0:T(8,128)(2,1)S(1)}, bf16[4,1040,128]{2,1,0:T(8,128)(2,1)S(1)}, u32[]{:S(2)}, u32[]{:S(2)}) %collective-permute-start.3) | collective-permute-done | bytes 1064992 | tf_op jit(solution)/shard_map/tiles_over_z/ppermute | solution.py:33
  39.9 2.1 collective-permute-start.5
  42.0 2.7 %collective-permute-start.8 = (bf16[193,16,128]{2,1,0:T(8,128)(2,1)S(1)}, bf16[193,16,128]{2,1,0:T(8,128)(2,1)S(1)}, u32[]{:S(2)}, u32[]{:S(2)}) collective-permute-start(bf16[193,16,128]{2,1,0:T(8,128)(2,1)S(1)} %get-tuple-element.54), channel_id=1, source_target_pairs={{0,2},{1,3},{2,0},{3,1},{4,6},{5,7},{6,4},{7,5},{8,10},{9,11},{10,... | collective-permute-start | bytes 2371592 | tf_op jit(solution)/shard_map/tiles_over_y/ppermute | solution.py:33
  44.7 19.8 %collective-permute-done.5.refs_3_ = bf16[4,1040,128]{2,1,0:T(8,128)(2,1)S(1)} collective-permute-done((bf16[4,1040,128]{2,1,0:T(8,128)(2,1)S(1)}, bf16[4,1040,128]{2,1,0:T(8,128)(2,1)S(1)}, u32[]{:S(2)}, u32[]{:S(2)}) %collective-permute-start.5) | collective-permute-done | bytes 1064992 | tf_op jit(solution)/shard_map/tiles_over_z/ppermute | solution.py:33
  65.3 6.9 %collective-permute-done.7.refs_1_.refs_6_ = bf16[193,16,128]{2,1,0:T(8,128)(2,1)S(1)} collective-permute-done((bf16[193,16,128]{2,1,0:T(8,128)(2,1)S(1)}, bf16[193,16,128]{2,1,0:T(8,128)(2,1)S(1)}, u32[]{:S(2)}, u32[]{:S(2)}) %collective-permute-start.7) | collective-permute-done | bytes 790560 | tf_op jit(solution)/shard_map/tiles_over_y/ppermute | solution.py:33
  72.3 3.7 %product.4 = bf16[4,4,2,128,256]{4,3,2,1,0:T(8,128)(2,1)S(1)} custom-call(s32[5]{0:T(128)S(1)} %stack.37.spot_ref.refs_0_, bf16[4,1040,128]{2,1,0:T(8,128)(2,1)S(1)} %stack.43.refs_0_.refs_1_, bf16[4,1040,128]{2,1,0:T(8,128)(2,1)S(1)} %gate.6.refs_2_, bf16[4,1040,128]{2,1,0:T(8,128)(2,1)S(1)} %collective-permute-done.5.refs_3_, ...), custom_call_target="tpu_custom_call" | custom-call | flops 2147483648 | bytes 6291456 | tf_op jit(solution)/shard_map/products/product/pallas_call | solution.py:51
  76.2 3.7 %product.5.refs_0_ = bf16[4,4,2,128,256]{4,3,2,1,0:T(8,128)(2,1)S(1)} custom-call(s32[5]{0:T(128)S(1)} %stack.37.spot_ref.refs_0_, bf16[4,1040,128]{2,1,0:T(8,128)(2,1)S(1)} %stack.43.refs_0_.refs_1_, bf16[4,1040,128]{2,1,0:T(8,128)(2,1)S(1)} %gate.6.refs_2_, bf16[4,1040,128]{2,1,0:T(8,128)(2,1)S(1)} %collective-permute-done.5.refs_3_, ...), custom_call_target="tpu_custom_call" | custom-call | flops 2147483648 | bytes 6291456 | tf_op jit(solution)/shard_map/products/product/pallas_call | solution.py:51
  80.0 12.4 %collective-permute-done.10.refs_0_ = bf16[4,1040,128]{2,1,0:T(8,128)(2,1)S(1)} collective-permute-done((bf16[4,1040,128]{2,1,0:T(8,128)(2,1)S(1)}, bf16[4,1040,128]{2,1,0:T(8,128)(2,1)S(1)}, u32[]{:S(2)}, u32[]{:S(2)}) %collective-permute-start.10) | collective-permute-done | bytes 1064992 | tf_op jit(solution)/shard_map/tiles_over_z/ppermute | solution.py:33
  95.6 1.6 collective-permute-start.11
  97.2 9.3 %collective-permute-done.12.refs_2_ = bf16[4,2,128,256]{3,2,1,0:T(8,128)(2,1)S(1)} collective-permute-done((bf16[4,2,128,256]{3,2,1,0:T(8,128)(2,1)S(1)}, bf16[4,2,128,256]{3,2,1,0:T(8,128)(2,1)S(1)}, u32[]{:S(2)}, u32[]{:S(2)}) %collective-permute-start.12) | collective-permute-done | bytes 524320 | tf_op jit(solution)/shard_map/sum_x/ppermute | solution.py:33
  107.5 8.5 %collective-permute-done.13.refs_3_ = bf16[4,2,128,256]{3,2,1,0:T(8,128)(2,1)S(1)} collective-permute-done((bf16[4,2,128,256]{3,2,1,0:T(8,128)(2,1)S(1)}, bf16[4,2,128,256]{3,2,1,0:T(8,128)(2,1)S(1)}, u32[]{:S(2)}, u32[]{:S(2)}) %collective-permute-start.13) | collective-permute-done | bytes 524320 | tf_op jit(solution)/shard_map/sum_x/ppermute | solution.py:33
  115.9 2.1 collective-permute-done.17.refs_3_
  118.7 3.7 %product.6 = bf16[4,4,2,128,256]{4,3,2,1,0:T(8,128)(2,1)S(1)} custom-call(s32[5]{0:T(128)S(1)} %stack.37.spot_ref.refs_0_, bf16[4,1040,128]{2,1,0:T(8,128)(2,1)S(1)} %stack.44.refs_0_.refs_1_, bf16[4,1040,128]{2,1,0:T(8,128)(2,1)S(1)} %gate.8.refs_2_, bf16[4,1040,128]{2,1,0:T(8,128)(2,1)S(1)} %collective-permute-done.17.refs_3_, ...), custom_call_target="tpu_custom_call" | custom-call | flops 2147483648 | bytes 6291456 | tf_op jit(solution)/shard_map/products/product/pallas_call | solution.py:51
  122.6 3.7 %product.7.refs_0_ = bf16[4,4,2,128,256]{4,3,2,1,0:T(8,128)(2,1)S(1)} custom-call(s32[5]{0:T(128)S(1)} %stack.37.spot_ref.refs_0_, bf16[4,1040,128]{2,1,0:T(8,128)(2,1)S(1)} %stack.44.refs_0_.refs_1_, bf16[4,1040,128]{2,1,0:T(8,128)(2,1)S(1)} %gate.8.refs_2_, bf16[4,1040,128]{2,1,0:T(8,128)(2,1)S(1)} %collective-permute-done.17.refs_3_, ...), custom_call_target="tpu_custom_call" | custom-call | flops 2147483648 | bytes 6291456 | tf_op jit(solution)/shard_map/products/product/pallas_call | solution.py:51
  127.0 2.5 %collective-permute-start.21 = (bf16[4,2,128,256]{3,2,1,0:T(8,128)(2,1)S(1)}, bf16[4,2,128,256]{3,2,1,0:T(8,128)(2,1)S(1)}, u32[]{:S(2)}, u32[]{:S(2)}) collective-permute-start(bf16[4,2,128,256]{3,2,1,0:T(8,128)(2,1)S(1)} %get-tuple-element.35), channel_id=1, source_target_pairs={{0,32},{1,33},{2,34},{3,35},{4,36},{5,37},{6,38},{7,39},{8,40},{9,... | collective-permute-start | bytes 1572872 | tf_op jit(solution)/shard_map/sum_x/ppermute | solution.py:33
  129.4 12.0 %collective-permute-done.21.refs_2_ = bf16[4,2,128,256]{3,2,1,0:T(8,128)(2,1)S(1)} collective-permute-done((bf16[4,2,128,256]{3,2,1,0:T(8,128)(2,1)S(1)}, bf16[4,2,128,256]{3,2,1,0:T(8,128)(2,1)S(1)}, u32[]{:S(2)}, u32[]{:S(2)}) %collective-permute-start.21) | collective-permute-done | bytes 524320 | tf_op jit(solution)/shard_map/sum_x/ppermute | solution.py:33
  141.7 3.8 %collective-permute-start.22 = (bf16[4,2,128,256]{3,2,1,0:T(8,128)(2,1)S(1)}, bf16[4,2,128,256]{3,2,1,0:T(8,128)(2,1)S(1)}, u32[]{:S(2)}, u32[]{:S(2)}) collective-permute-start(bf16[4,2,128,256]{3,2,1,0:T(8,128)(2,1)S(1)} %relay.3), channel_id=1, source_target_pairs={{0,32},{1,33},{2,34},{3,35},{4,36},{5,37},{6,38},{7,39},{8,40},{9,... | collective-permute-start | bytes 1572872 | tf_op jit(solution)/shard_map/sum_x/ppermute | solution.py:33
  146.1 1.7 collective-permute-start.16
  147.8 4.3 %collective-permute-done.22.refs_3_ = bf16[4,2,128,256]{3,2,1,0:T(8,128)(2,1)S(1)} collective-permute-done((bf16[4,2,128,256]{3,2,1,0:T(8,128)(2,1)S(1)}, bf16[4,2,128,256]{3,2,1,0:T(8,128)(2,1)S(1)}, u32[]{:S(2)}, u32[]{:S(2)}) %collective-permute-start.22) | collective-permute-done | bytes 524320 | tf_op jit(solution)/shard_map/sum_x/ppermute | solution.py:33
  154.7 2.5 %collective-permute-start.26 = (bf16[2,2,16,2048]{3,2,1,0:T(8,128)(2,1)S(1)}, bf16[2,2,16,2048]{3,2,1,0:T(8,128)(2,1)S(1)}, u32[]{:S(2)}, u32[]{:S(2)}) collective-permute-start(bf16[2,2,16,2048]{3,2,1,0:T(8,128)(2,1)S(1)} %get-tuple-element.41), channel_id=1, source_target_pairs={{0,32},{1,33},{2,34},{3,35},{4,36},{5,37},{6,38},{7,39},{8,40},{9,... | collective-permute-start | bytes 786440 | tf_op jit(solution)/shard_map/exchange_over_row/ppermute | solution.py:33
  157.4 1.8 collective-permute-start.25
  159.2 7.8 %collective-permute-done.26.refs_2_ = bf16[2,2,16,2048]{3,2,1,0:T(8,128)(2,1)S(1)} collective-permute-done((bf16[2,2,16,2048]{3,2,1,0:T(8,128)(2,1)S(1)}, bf16[2,2,16,2048]{3,2,1,0:T(8,128)(2,1)S(1)}, u32[]{:S(2)}, u32[]{:S(2)}) %collective-permute-start.26) | collective-permute-done | bytes 262176 | tf_op jit(solution)/shard_map/exchange_over_row/ppermute | solution.py:33
  168.1 3.1 %collective-permute-start.31 = (bf16[2,2,16,2048]{3,2,1,0:T(8,128)(2,1)S(1)}, bf16[2,2,16,2048]{3,2,1,0:T(8,128)(2,1)S(1)}, u32[]{:S(2)}, u32[]{:S(2)}) collective-permute-start(bf16[2,2,16,2048]{3,2,1,0:T(8,128)(2,1)S(1)} %get-tuple-element.49), channel_id=1, source_target_pairs={{0,96},{1,97},{2,98},{3,99},{4,100},{5,101},{6,102},{7,103},{8,104... | collective-permute-start | bytes 786440 | tf_op jit(solution)/shard_map/exchange_over_row/ppermute | solution.py:33
  171.2 3.6 %collective-permute-start.30 = (bf16[2,2,16,2048]{3,2,1,0:T(8,128)(2,1)S(1)}, bf16[2,2,16,2048]{3,2,1,0:T(8,128)(2,1)S(1)}, u32[]{:S(2)}, u32[]{:S(2)}) collective-permute-start(bf16[2,2,16,2048]{3,2,1,0:T(8,128)(2,1)S(1)} %get-tuple-element.48), channel_id=1, source_target_pairs={{0,64},{1,65},{2,66},{3,67},{4,68},{5,69},{6,70},{7,71},{8,72},{9,... | collective-permute-start | bytes 786440 | tf_op jit(solution)/shard_map/exchange_over_row/ppermute | solution.py:33
  174.8 1.6 collective-permute-start.29
  176.5 3.0 %collective-permute-done.28.refs_4_ = bf16[2,2,16,2048]{3,2,1,0:T(8,128)(2,1)S(1)} collective-permute-done((bf16[2,2,16,2048]{3,2,1,0:T(8,128)(2,1)S(1)}, bf16[2,2,16,2048]{3,2,1,0:T(8,128)(2,1)S(1)}, u32[]{:S(2)}, u32[]{:S(2)}) %collective-permute-start.28) | collective-permute-done | bytes 262176 | tf_op jit(solution)/shard_map/exchange_over_row/ppermute | solution.py:33
  179.5 2.8 %collective-permute-done.31.refs_8_ = bf16[2,2,16,2048]{3,2,1,0:T(8,128)(2,1)S(1)} collective-permute-done((bf16[2,2,16,2048]{3,2,1,0:T(8,128)(2,1)S(1)}, bf16[2,2,16,2048]{3,2,1,0:T(8,128)(2,1)S(1)}, u32[]{:S(2)}, u32[]{:S(2)}) %collective-permute-start.31) | collective-permute-done | bytes 262176 | tf_op jit(solution)/shard_map/exchange_over_row/ppermute | solution.py:33
  182.3 2.8 %collective-permute-done.30.refs_7_ = bf16[2,2,16,2048]{3,2,1,0:T(8,128)(2,1)S(1)} collective-permute-done((bf16[2,2,16,2048]{3,2,1,0:T(8,128)(2,1)S(1)}, bf16[2,2,16,2048]{3,2,1,0:T(8,128)(2,1)S(1)}, u32[]{:S(2)}, u32[]{:S(2)}) %collective-permute-start.30) | collective-permute-done | bytes 262176 | tf_op jit(solution)/shard_map/exchange_over_row/ppermute | solution.py:33
  185.4 2.6 %collective-permute-done.32.refs_9_ = bf16[4,2,16,4096]{3,2,1,0:T(8,128)(2,1)S(1)} collective-permute-done((bf16[4,2,16,4096]{3,2,1,0:T(8,128)(2,1)S(1)}, bf16[4,2,16,4096]{3,2,1,0:T(8,128)(2,1)S(1)}, u32[]{:S(2)}, u32[]{:S(2)}) %collective-permute-start.32) | collective-permute-done | bytes 1048608 | tf_op jit(solution)/shard_map/exchange/ppermute | solution.py:42
  188.0 2.0 exchange.1
  190.1 3.2 %collective-permute-start.33 = (f32[32,128]{1,0:T(8,128)S(1)}, f32[32,128]{1,0:T(8,128)S(1)}, u32[]{:S(2)}, u32[]{:S(2)}) collective-permute-start(f32[32,128]{1,0:T(8,128)S(1)} %get-tuple-element.51), channel_id=1, source_target_pairs={{0,32},{1,33},{2,34},{3,35},{4,36},{5,37},{6,38},{7,39},{8,40},{9,... | collective-permute-start | bytes 49160 | tf_op jit(solution)/shard_map/exchange/ppermute | solution.py:33
  193.3 1.7 collective-permute-done.35
  195.1 3.5 %collective-permute-done.34 = f32[32,128]{1,0:T(8,128)S(1)} collective-permute-done((f32[32,128]{1,0:T(8,128)S(1)}, f32[32,128]{1,0:T(8,128)S(1)}, u32[]{:S(2)}, u32[]{:S(2)}) %collective-permute-start.34) | collective-permute-done | bytes 16416 | tf_op jit(solution)/shard_map/exchange/ppermute | solution.py:33
  199.9 3.7 %collective-permute-done.37 = f32[2,16,128]{2,1,0:T(8,128)S(1)} collective-permute-done((f32[2,16,128]{2,1,0:T(8,128)S(1)}, f32[2,16,128]{2,1,0:T(8,128)S(1)}, u32[]{:S(2)}, u32[]{:S(2)}) %collective-permute-start.37) | collective-permute-done | bytes 16416 | tf_op jit(solution)/shard_map/exchange/ppermute | solution.py:38
  203.8 5.1 %collective-permute-done.38 = f32[2,16,128]{2,1,0:T(8,128)S(1)} collective-permute-done((f32[2,16,128]{2,1,0:T(8,128)S(1)}, f32[2,16,128]{2,1,0:T(8,128)S(1)}, u32[]{:S(2)}, u32[]{:S(2)}) %collective-permute-start.38) | collective-permute-done | bytes 16416 | tf_op jit(solution)/shard_map/exchange/ppermute | solution.py:38
  208.9 1.5 collective-permute-start.39
  210.4 2.3 %collective-permute-done.39 = f32[2,16,128]{2,1,0:T(8,128)S(1)} collective-permute-done((f32[2,16,128]{2,1,0:T(8,128)S(1)}, f32[2,16,128]{2,1,0:T(8,128)S(1)}, u32[]{:S(2)}, u32[]{:S(2)}) %collective-permute-start.39) | collective-permute-done | bytes 16416 | tf_op jit(solution)/shard_map/exchange/ppermute | solution.py:38
  212.7 2.8 %collective-permute-start.40 = (f32[2,16,128]{2,1,0:T(8,128)S(1)}, f32[2,16,128]{2,1,0:T(8,128)S(1)}, u32[]{:S(2)}, u32[]{:S(2)}) collective-permute-start(f32[2,16,128]{2,1,0:T(8,128)S(1)} %add.41), channel_id=1, source_target_pairs={{0,8},{1,9},{2,10},{3,11},{4,12},{5,13},{6,14},{7,15},{8,0},{9,1},... | collective-permute-start | bytes 49160 | tf_op jit(solution)/shard_map/exchange/ppermute | solution.py:38
  215.4 2.5 %assemble.1 = bf16[2,64,16,256]{3,2,1,0:T(8,128)(2,1)} custom-call(bf16[2,64,2048]{2,1,0:T(8,128)(2,1)S(1)} %get-tuple-element.37.refs_0_, bf16[2,64,2048]{2,1,0:T(8,128)(2,1)S(1)} %get-tuple-element.43.refs_1_), custom_call_target="tpu_custom_call" | custom-call | bytes 2097152 | tf_op jit(solution)/shard_map/fitted_out/assemble/pallas_call | solution.py:51
  (109 shorter events, 17.3 us)
Async XLA Ops:
  2.0 1.6 copy-start.1
  3.6 8.0 %copy-start = (bf16[1024,256]{1,0:T(8,128)(2,1)S(1)}, bf16[1024,256]{1,0:T(8,128)(2,1)}, u32[]{:S(2)}) copy-start(bf16[1024,256]{1,0:T(8,128)(2,1)} %refs_5_.9) | copy-start | bytes 1572868
  3.6 8.0 %copy-start.2 = (bf16[1,64,128,128]{3,2,1,0:T(8,128)(2,1)S(1)}, bf16[1,64,128,128]{3,2,1,0:T(8,128)(2,1)}, u32[]{:S(2)}) copy-start(bf16[1,64,128,128]{3,2,1,0:T(8,128)(2,1)} %param.5) | copy-start | bytes 6291460
  5.7 10.4 %collective-permute-start = (bf16[65,16,128]{2,1,0:T(8,128)(2,1)S(1)}, bf16[65,16,128]{2,1,0:T(8,128)(2,1)S(1)}, u32[]{:S(2)}, u32[]{:S(2)}) collective-permute-start(bf16[65,16,128]{2,1,0:T(8,128)(2,1)S(1)} %get-tuple-element.59), channel_id=1, source_target_pairs={{0,1},{1,2},{2,3},{3,0},{4,5},{5,6},{6,7},{7,4},{8,9},{9,10},{10,1... | collective-permute-start | bytes 798728 | tf_op jit(solution)/shard_map/tiles_over_y/ppermute | solution.py:33
  7.4 15.2 %collective-permute-start.1 = (bf16[65,16,128]{2,1,0:T(8,128)(2,1)S(1)}, bf16[65,16,128]{2,1,0:T(8,128)(2,1)S(1)}, u32[]{:S(2)}, u32[]{:S(2)}) collective-permute-start(bf16[65,16,128]{2,1,0:T(8,128)(2,1)S(1)} %get-tuple-element.58), channel_id=1, source_target_pairs={{0,2},{1,3},{2,0},{3,1},{4,6},{5,7},{6,4},{7,5},{8,10},{9,11},{10,... | collective-permute-start | bytes 798728 | tf_op jit(solution)/shard_map/tiles_over_y/ppermute | solution.py:33
  10.3 12.3 %collective-permute-start.2 = (bf16[65,16,128]{2,1,0:T(8,128)(2,1)S(1)}, bf16[65,16,128]{2,1,0:T(8,128)(2,1)S(1)}, u32[]{:S(2)}, u32[]{:S(2)}) collective-permute-start(bf16[65,16,128]{2,1,0:T(8,128)(2,1)S(1)} %get-tuple-element.57), channel_id=1, source_target_pairs={{0,3},{1,0},{2,1},{3,2},{4,7},{5,4},{6,5},{7,6},{8,11},{9,8},{10,9... | collective-permute-start | bytes 798728 | tf_op jit(solution)/shard_map/tiles_over_y/ppermute | solution.py:33
  22.7 17.1 %collective-permute-start.3 = (bf16[4,1040,128]{2,1,0:T(8,128)(2,1)S(1)}, bf16[4,1040,128]{2,1,0:T(8,128)(2,1)S(1)}, u32[]{:S(2)}, u32[]{:S(2)}) collective-permute-start(bf16[4,1040,128]{2,1,0:T(8,128)(2,1)S(1)} %stack.43.refs_0_.refs_1_), channel_id=1, source_target_pairs={{0,4},{1,5},{2,6},{3,7},{4,8},{5,9},{6,10},{7,11},{8,12},{9,13},{1... | collective-permute-start | bytes 3194888 | tf_op jit(solution)/shard_map/tiles_over_z/ppermute | solution.py:33
  25.3 12.1 %collective-permute-start.4 = (bf16[193,16,128]{2,1,0:T(8,128)(2,1)S(1)}, bf16[193,16,128]{2,1,0:T(8,128)(2,1)S(1)}, u32[]{:S(2)}, u32[]{:S(2)}) collective-permute-start(bf16[193,16,128]{2,1,0:T(8,128)(2,1)S(1)} %get-tuple-element.56), channel_id=1, source_target_pairs={{0,3},{1,0},{2,1},{3,2},{4,7},{5,4},{6,5},{7,6},{8,11},{9,8},{10,9... | collective-permute-start | bytes 2371592 | tf_op jit(solution)/shard_map/tiles_over_y/ppermute | solution.py:33
  39.9 24.6 %collective-permute-start.5 = (bf16[4,1040,128]{2,1,0:T(8,128)(2,1)S(1)}, bf16[4,1040,128]{2,1,0:T(8,128)(2,1)S(1)}, u32[]{:S(2)}, u32[]{:S(2)}) collective-permute-start(bf16[4,1040,128]{2,1,0:T(8,128)(2,1)S(1)} %gate.7), channel_id=1, source_target_pairs={{0,12},{1,13},{2,14},{3,15},{4,0},{5,1},{6,2},{7,3},{8,4},{9,5},{1... | collective-permute-start | bytes 3194888 | tf_op jit(solution)/shard_map/tiles_over_z/ppermute | solution.py:33
  42.0 23.3 %collective-permute-start.6 = (bf16[4,1040,128]{2,1,0:T(8,128)(2,1)S(1)}, bf16[4,1040,128]{2,1,0:T(8,128)(2,1)S(1)}, u32[]{:S(2)}, u32[]{:S(2)}) collective-permute-start(bf16[4,1040,128]{2,1,0:T(8,128)(2,1)S(1)} %gate.6.refs_2_), channel_id=1, source_target_pairs={{0,4},{1,5},{2,6},{3,7},{4,8},{5,9},{6,10},{7,11},{8,12},{9,13},{1... | collective-permute-start | bytes 3194888 | tf_op jit(solution)/shard_map/tiles_over_z/ppermute | solution.py:33
  42.0 30.2 %collective-permute-start.7 = (bf16[193,16,128]{2,1,0:T(8,128)(2,1)S(1)}, bf16[193,16,128]{2,1,0:T(8,128)(2,1)S(1)}, u32[]{:S(2)}, u32[]{:S(2)}) collective-permute-start(bf16[193,16,128]{2,1,0:T(8,128)(2,1)S(1)} %get-tuple-element.55), channel_id=1, source_target_pairs={{0,1},{1,2},{2,3},{3,0},{4,5},{5,6},{6,7},{7,4},{8,9},{9,10},{10,1... | collective-permute-start | bytes 2371592 | tf_op jit(solution)/shard_map/tiles_over_y/ppermute | solution.py:33
  42.0 30.2 %collective-permute-start.8 = (bf16[193,16,128]{2,1,0:T(8,128)(2,1)S(1)}, bf16[193,16,128]{2,1,0:T(8,128)(2,1)S(1)}, u32[]{:S(2)}, u32[]{:S(2)}) collective-permute-start(bf16[193,16,128]{2,1,0:T(8,128)(2,1)S(1)} %get-tuple-element.54), channel_id=1, source_target_pairs={{0,2},{1,3},{2,0},{3,1},{4,6},{5,7},{6,4},{7,5},{8,10},{9,11},{10,... | collective-permute-start | bytes 2371592 | tf_op jit(solution)/shard_map/tiles_over_y/ppermute | solution.py:33
  76.0 16.4 %collective-permute-start.9 = (bf16[4,4,2,128,256]{4,3,2,1,0:T(8,128)(2,1)S(1)}, bf16[4,4,2,128,256]{4,3,2,1,0:T(8,128)(2,1)S(1)}, u32[]{:S(2)}, u32[]{:S(2)}) collective-permute-start(bf16[4,4,2,128,256]{4,3,2,1,0:T(8,128)(2,1)S(1)} %product.4), channel_id=1, source_target_pairs={{0,16},{16,0},{32,48},{48,32},{64,80},{80,64},{96,112},{112,96},{1... | collective-permute-start | bytes 6291464 | tf_op jit(solution)/shard_map/sum_cores/ppermute | solution.py:42
  76.1 16.3 %collective-permute-start.10 = (bf16[4,1040,128]{2,1,0:T(8,128)(2,1)S(1)}, bf16[4,1040,128]{2,1,0:T(8,128)(2,1)S(1)}, u32[]{:S(2)}, u32[]{:S(2)}) collective-permute-start(bf16[4,1040,128]{2,1,0:T(8,128)(2,1)S(1)} %stack.44.refs_0_.refs_1_), channel_id=1, source_target_pairs={{0,4},{1,5},{2,6},{3,7},{4,8},{5,9},{6,10},{7,11},{8,12},{9,13},{1... | collective-permute-start | bytes 3194888 | tf_op jit(solution)/shard_map/tiles_over_z/ppermute | solution.py:33
  92.7 13.8 %collective-permute-start.12 = (bf16[4,2,128,256]{3,2,1,0:T(8,128)(2,1)S(1)}, bf16[4,2,128,256]{3,2,1,0:T(8,128)(2,1)S(1)}, u32[]{:S(2)}, u32[]{:S(2)}) collective-permute-start(bf16[4,2,128,256]{3,2,1,0:T(8,128)(2,1)S(1)} %get-tuple-element.29), channel_id=1, source_target_pairs={{0,32},{1,33},{2,34},{3,35},{4,36},{5,37},{6,38},{7,39},{8,40},{9,... | collective-permute-start | bytes 1572872 | tf_op jit(solution)/shard_map/sum_x/ppermute | solution.py:33
  93.3 24.7 %collective-permute-start.17 = (bf16[4,1040,128]{2,1,0:T(8,128)(2,1)S(1)}, bf16[4,1040,128]{2,1,0:T(8,128)(2,1)S(1)}, u32[]{:S(2)}, u32[]{:S(2)}) collective-permute-start(bf16[4,1040,128]{2,1,0:T(8,128)(2,1)S(1)} %gate.9), channel_id=1, source_target_pairs={{0,12},{1,13},{2,14},{3,15},{4,0},{5,1},{6,2},{7,3},{8,4},{9,5},{1... | collective-permute-start | bytes 3194888 | tf_op jit(solution)/shard_map/tiles_over_z/ppermute | solution.py:33
  94.5 24.2 %collective-permute-start.18 = (bf16[4,1040,128]{2,1,0:T(8,128)(2,1)S(1)}, bf16[4,1040,128]{2,1,0:T(8,128)(2,1)S(1)}, u32[]{:S(2)}, u32[]{:S(2)}) collective-permute-start(bf16[4,1040,128]{2,1,0:T(8,128)(2,1)S(1)} %gate.8.refs_2_), channel_id=1, source_target_pairs={{0,4},{1,5},{2,6},{3,7},{4,8},{5,9},{6,10},{7,11},{8,12},{9,13},{1... | collective-permute-start | bytes 3194888 | tf_op jit(solution)/shard_map/tiles_over_z/ppermute | solution.py:33
  95.6 11.8 %collective-permute-start.11 = (bf16[4,2,128,256]{3,2,1,0:T(8,128)(2,1)S(1)}, bf16[4,2,128,256]{3,2,1,0:T(8,128)(2,1)S(1)}, u32[]{:S(2)}, u32[]{:S(2)}) collective-permute-start(bf16[4,2,128,256]{3,2,1,0:T(8,128)(2,1)S(1)} %get-tuple-element.28), channel_id=1, source_target_pairs={{0,96},{1,97},{2,98},{3,99},{4,100},{5,101},{6,102},{7,103},{8,104... | collective-permute-start | bytes 1572872 | tf_op jit(solution)/shard_map/sum_x/ppermute | solution.py:33
  106.7 9.2 %collective-permute-start.13 = (bf16[4,2,128,256]{3,2,1,0:T(8,128)(2,1)S(1)}, bf16[4,2,128,256]{3,2,1,0:T(8,128)(2,1)S(1)}, u32[]{:S(2)}, u32[]{:S(2)}) collective-permute-start(bf16[4,2,128,256]{3,2,1,0:T(8,128)(2,1)S(1)} %relay.2), channel_id=1, source_target_pairs={{0,32},{1,33},{2,34},{3,35},{4,36},{5,37},{6,38},{7,39},{8,40},{9,... | collective-permute-start | bytes 1572872 | tf_op jit(solution)/shard_map/sum_x/ppermute | solution.py:33
  122.5 4.2 %collective-permute-start.19 = (bf16[4,4,2,128,256]{4,3,2,1,0:T(8,128)(2,1)S(1)}, bf16[4,4,2,128,256]{4,3,2,1,0:T(8,128)(2,1)S(1)}, u32[]{:S(2)}, u32[]{:S(2)}) collective-permute-start(bf16[4,4,2,128,256]{4,3,2,1,0:T(8,128)(2,1)S(1)} %product.6), channel_id=1, source_target_pairs={{0,16},{16,0},{32,48},{48,32},{64,80},{80,64},{96,112},{112,96},{1... | collective-permute-start | bytes 6291464 | tf_op jit(solution)/shard_map/sum_cores/ppermute | solution.py:42
  127.0 14.5 %collective-permute-start.21 = (bf16[4,2,128,256]{3,2,1,0:T(8,128)(2,1)S(1)}, bf16[4,2,128,256]{3,2,1,0:T(8,128)(2,1)S(1)}, u32[]{:S(2)}, u32[]{:S(2)}) collective-permute-start(bf16[4,2,128,256]{3,2,1,0:T(8,128)(2,1)S(1)} %get-tuple-element.35), channel_id=1, source_target_pairs={{0,32},{1,33},{2,34},{3,35},{4,36},{5,37},{6,38},{7,39},{8,40},{9,... | collective-permute-start | bytes 1572872 | tf_op jit(solution)/shard_map/sum_x/ppermute | solution.py:33
  129.4 18.3 %collective-permute-start.20 = (bf16[4,2,128,256]{3,2,1,0:T(8,128)(2,1)S(1)}, bf16[4,2,128,256]{3,2,1,0:T(8,128)(2,1)S(1)}, u32[]{:S(2)}, u32[]{:S(2)}) collective-permute-start(bf16[4,2,128,256]{3,2,1,0:T(8,128)(2,1)S(1)} %get-tuple-element.34), channel_id=1, source_target_pairs={{0,96},{1,97},{2,98},{3,99},{4,100},{5,101},{6,102},{7,103},{8,104... | collective-permute-start | bytes 1572872 | tf_op jit(solution)/shard_map/sum_x/ppermute | solution.py:33
  141.7 10.5 %collective-permute-start.22 = (bf16[4,2,128,256]{3,2,1,0:T(8,128)(2,1)S(1)}, bf16[4,2,128,256]{3,2,1,0:T(8,128)(2,1)S(1)}, u32[]{:S(2)}, u32[]{:S(2)}) collective-permute-start(bf16[4,2,128,256]{3,2,1,0:T(8,128)(2,1)S(1)} %relay.3), channel_id=1, source_target_pairs={{0,32},{1,33},{2,34},{3,35},{4,36},{5,37},{6,38},{7,39},{8,40},{9,... | collective-permute-start | bytes 1572872 | tf_op jit(solution)/shard_map/sum_x/ppermute | solution.py:33
  145.7 6.7 %collective-permute-start.14 = (bf16[2,128,256]{2,1,0:T(8,128)(2,1)S(1)}, bf16[2,128,256]{2,1,0:T(8,128)(2,1)S(1)}, u32[]{:S(2)}, u32[]{:S(2)}) collective-permute-start(bf16[2,128,256]{2,1,0:T(8,128)(2,1)S(1)} %get-tuple-element.31), channel_id=1, source_target_pairs={{0,3},{1,0},{2,1},{3,2},{4,7},{5,4},{6,5},{7,6},{8,11},{9,8},{10,9... | collective-permute-start | bytes 393224 | tf_op jit(solution)/shard_map/coeffs_over_y/ppermute | solution.py:33
  145.8 6.7 %collective-permute-start.15 = (bf16[2,128,256]{2,1,0:T(8,128)(2,1)S(1)}, bf16[2,128,256]{2,1,0:T(8,128)(2,1)S(1)}, u32[]{:S(2)}, u32[]{:S(2)}) collective-permute-start(bf16[2,128,256]{2,1,0:T(8,128)(2,1)S(1)} %get-tuple-element.32), channel_id=1, source_target_pairs={{0,2},{1,3},{2,0},{3,1},{4,6},{5,7},{6,4},{7,5},{8,10},{9,11},{10,... | collective-permute-start | bytes 393224 | tf_op jit(solution)/shard_map/coeffs_over_y/ppermute | solution.py:33
  146.1 7.7 %copy-start.3 = (f32[2,64,64]{2,1,0:T(8,128)S(1)}, f32[2,64,64]{2,1,0:T(8,128)}, u32[]{:S(2)}) copy-start(f32[2,64,64]{2,1,0:T(8,128)} %refs_5_.11) | copy-start | bytes 98308
  146.1 7.7 %collective-permute-start.16 = (bf16[2,128,256]{2,1,0:T(8,128)(2,1)S(1)}, bf16[2,128,256]{2,1,0:T(8,128)(2,1)S(1)}, u32[]{:S(2)}, u32[]{:S(2)}) collective-permute-start(bf16[2,128,256]{2,1,0:T(8,128)(2,1)S(1)} %get-tuple-element.33), channel_id=1, source_target_pairs={{0,1},{1,2},{2,3},{3,0},{4,5},{5,6},{6,7},{7,4},{8,9},{9,10},{10,1... | collective-permute-start | bytes 393224 | tf_op jit(solution)/shard_map/coeffs_over_y/ppermute | solution.py:33
  154.7 12.4 %collective-permute-start.26 = (bf16[2,2,16,2048]{3,2,1,0:T(8,128)(2,1)S(1)}, bf16[2,2,16,2048]{3,2,1,0:T(8,128)(2,1)S(1)}, u32[]{:S(2)}, u32[]{:S(2)}) collective-permute-start(bf16[2,2,16,2048]{3,2,1,0:T(8,128)(2,1)S(1)} %get-tuple-element.41), channel_id=1, source_target_pairs={{0,32},{1,33},{2,34},{3,35},{4,36},{5,37},{6,38},{7,39},{8,40},{9,... | collective-permute-start | bytes 786440 | tf_op jit(solution)/shard_map/exchange_over_row/ppermute | solution.py:33
  157.2 9.9 %collective-permute-start.23 = (bf16[2,128,256]{2,1,0:T(8,128)(2,1)S(1)}, bf16[2,128,256]{2,1,0:T(8,128)(2,1)S(1)}, u32[]{:S(2)}, u32[]{:S(2)}) collective-permute-start(bf16[2,128,256]{2,1,0:T(8,128)(2,1)S(1)} %get-tuple-element.38), channel_id=1, source_target_pairs={{0,3},{1,0},{2,1},{3,2},{4,7},{5,4},{6,5},{7,6},{8,11},{9,8},{10,9... | collective-permute-start | bytes 393224 | tf_op jit(solution)/shard_map/coeffs_over_y/ppermute | solution.py:33
  157.2 9.9 %collective-permute-start.24 = (bf16[2,128,256]{2,1,0:T(8,128)(2,1)S(1)}, bf16[2,128,256]{2,1,0:T(8,128)(2,1)S(1)}, u32[]{:S(2)}, u32[]{:S(2)}) collective-permute-start(bf16[2,128,256]{2,1,0:T(8,128)(2,1)S(1)} %get-tuple-element.39), channel_id=1, source_target_pairs={{0,2},{1,3},{2,0},{3,1},{4,6},{5,7},{6,4},{7,5},{8,10},{9,11},{10,... | collective-permute-start | bytes 393224 | tf_op jit(solution)/shard_map/coeffs_over_y/ppermute | solution.py:33
  157.4 9.7 %collective-permute-start.25 = (bf16[2,128,256]{2,1,0:T(8,128)(2,1)S(1)}, bf16[2,128,256]{2,1,0:T(8,128)(2,1)S(1)}, u32[]{:S(2)}, u32[]{:S(2)}) collective-permute-start(bf16[2,128,256]{2,1,0:T(8,128)(2,1)S(1)} %get-tuple-element.40), channel_id=1, source_target_pairs={{0,1},{1,2},{2,3},{3,0},{4,5},{5,6},{6,7},{7,4},{8,9},{9,10},{10,1... | collective-permute-start | bytes 393224 | tf_op jit(solution)/shard_map/coeffs_over_y/ppermute | solution.py:33
  159.2 7.9 %collective-permute-start.27 = (bf16[2,2,16,2048]{3,2,1,0:T(8,128)(2,1)S(1)}, bf16[2,2,16,2048]{3,2,1,0:T(8,128)(2,1)S(1)}, u32[]{:S(2)}, u32[]{:S(2)}) collective-permute-start(bf16[2,2,16,2048]{3,2,1,0:T(8,128)(2,1)S(1)} %get-tuple-element.42), channel_id=1, source_target_pairs={{0,64},{1,65},{2,66},{3,67},{4,68},{5,69},{6,70},{7,71},{8,72},{9,... | collective-permute-start | bytes 786440 | tf_op jit(solution)/shard_map/exchange_over_row/ppermute | solution.py:33
  167.0 12.5 %collective-permute-start.28 = (bf16[2,2,16,2048]{3,2,1,0:T(8,128)(2,1)S(1)}, bf16[2,2,16,2048]{3,2,1,0:T(8,128)(2,1)S(1)}, u32[]{:S(2)}, u32[]{:S(2)}) collective-permute-start(bf16[2,2,16,2048]{3,2,1,0:T(8,128)(2,1)S(1)} %get-tuple-element.45), channel_id=1, source_target_pairs={{0,96},{1,97},{2,98},{3,99},{4,100},{5,101},{6,102},{7,103},{8,104... | collective-permute-start | bytes 786440 | tf_op jit(solution)/shard_map/exchange_over_row/ppermute | solution.py:33
  168.1 14.2 %collective-permute-start.31 = (bf16[2,2,16,2048]{3,2,1,0:T(8,128)(2,1)S(1)}, bf16[2,2,16,2048]{3,2,1,0:T(8,128)(2,1)S(1)}, u32[]{:S(2)}, u32[]{:S(2)}) collective-permute-start(bf16[2,2,16,2048]{3,2,1,0:T(8,128)(2,1)S(1)} %get-tuple-element.49), channel_id=1, source_target_pairs={{0,96},{1,97},{2,98},{3,99},{4,100},{5,101},{6,102},{7,103},{8,104... | collective-permute-start | bytes 786440 | tf_op jit(solution)/shard_map/exchange_over_row/ppermute | solution.py:33
  171.2 13.9 %collective-permute-start.30 = (bf16[2,2,16,2048]{3,2,1,0:T(8,128)(2,1)S(1)}, bf16[2,2,16,2048]{3,2,1,0:T(8,128)(2,1)S(1)}, u32[]{:S(2)}, u32[]{:S(2)}) collective-permute-start(bf16[2,2,16,2048]{3,2,1,0:T(8,128)(2,1)S(1)} %get-tuple-element.48), channel_id=1, source_target_pairs={{0,64},{1,65},{2,66},{3,67},{4,68},{5,69},{6,70},{7,71},{8,72},{9,... | collective-permute-start | bytes 786440 | tf_op jit(solution)/shard_map/exchange_over_row/ppermute | solution.py:33
  174.8 10.4 %collective-permute-start.29 = (bf16[2,2,16,2048]{3,2,1,0:T(8,128)(2,1)S(1)}, bf16[2,2,16,2048]{3,2,1,0:T(8,128)(2,1)S(1)}, u32[]{:S(2)}, u32[]{:S(2)}) collective-permute-start(bf16[2,2,16,2048]{3,2,1,0:T(8,128)(2,1)S(1)} %get-tuple-element.47), channel_id=1, source_target_pairs={{0,32},{1,33},{2,34},{3,35},{4,36},{5,37},{6,38},{7,39},{8,40},{9,... | collective-permute-start | bytes 786440 | tf_op jit(solution)/shard_map/exchange_over_row/ppermute | solution.py:33
  185.3 2.7 %collective-permute-start.32 = (bf16[4,2,16,4096]{3,2,1,0:T(8,128)(2,1)S(1)}, bf16[4,2,16,4096]{3,2,1,0:T(8,128)(2,1)S(1)}, u32[]{:S(2)}, u32[]{:S(2)}) collective-permute-start(bf16[4,2,16,4096]{3,2,1,0:T(8,128)(2,1)S(1)} %maximum_maximum_fusion), channel_id=1, source_target_pairs={{0,16},{16,0},{32,48},{48,32},{64,80},{80,64},{96,112},{112,96},{1... | collective-permute-start | bytes 3145736 | tf_op jit(solution)/shard_map/exchange/ppermute | solution.py:42
  190.0 5.0 %collective-permute-start.35 = (f32[32,128]{1,0:T(8,128)S(1)}, f32[32,128]{1,0:T(8,128)S(1)}, u32[]{:S(2)}, u32[]{:S(2)}) collective-permute-start(f32[32,128]{1,0:T(8,128)S(1)} %get-tuple-element.53), channel_id=1, source_target_pairs={{0,96},{1,97},{2,98},{3,99},{4,100},{5,101},{6,102},{7,103},{8,104... | collective-permute-start | bytes 49160 | tf_op jit(solution)/shard_map/exchange/ppermute | solution.py:33
  190.1 4.9 %collective-permute-start.33 = (f32[32,128]{1,0:T(8,128)S(1)}, f32[32,128]{1,0:T(8,128)S(1)}, u32[]{:S(2)}, u32[]{:S(2)}) collective-permute-start(f32[32,128]{1,0:T(8,128)S(1)} %get-tuple-element.51), channel_id=1, source_target_pairs={{0,32},{1,33},{2,34},{3,35},{4,36},{5,37},{6,38},{7,39},{8,40},{9,... | collective-permute-start | bytes 49160 | tf_op jit(solution)/shard_map/exchange/ppermute | solution.py:33
  193.3 5.2 %collective-permute-start.34 = (f32[32,128]{1,0:T(8,128)S(1)}, f32[32,128]{1,0:T(8,128)S(1)}, u32[]{:S(2)}, u32[]{:S(2)}) collective-permute-start(f32[32,128]{1,0:T(8,128)S(1)} %get-tuple-element.52), channel_id=1, source_target_pairs={{0,64},{1,65},{2,66},{3,67},{4,68},{5,69},{6,70},{7,71},{8,72},{9,... | collective-permute-start | bytes 49160 | tf_op jit(solution)/shard_map/exchange/ppermute | solution.py:33
  198.6 1.3 collective-permute-start.36
  199.9 3.8 %collective-permute-start.37 = (f32[2,16,128]{2,1,0:T(8,128)S(1)}, f32[2,16,128]{2,1,0:T(8,128)S(1)}, u32[]{:S(2)}, u32[]{:S(2)}) collective-permute-start(f32[2,16,128]{2,1,0:T(8,128)S(1)} %pad_maximum_fusion), channel_id=1, source_target_pairs={{0,1},{1,0},{2,3},{3,2},{4,5},{5,4},{6,7},{7,6},{8,9},{9,8},{10,11... | collective-permute-start | bytes 49160 | tf_op jit(solution)/shard_map/exchange/ppermute | solution.py:38
  203.7 5.2 %collective-permute-start.38 = (f32[2,16,128]{2,1,0:T(8,128)S(1)}, f32[2,16,128]{2,1,0:T(8,128)S(1)}, u32[]{:S(2)}, u32[]{:S(2)}) collective-permute-start(f32[2,16,128]{2,1,0:T(8,128)S(1)} %fusion), channel_id=1, source_target_pairs={{0,2},{1,3},{2,0},{3,1},{4,6},{5,7},{6,4},{7,5},{8,10},{9,11},{10,... | collective-permute-start | bytes 49160 | tf_op jit(solution)/shard_map/exchange/ppermute | solution.py:38
  208.9 3.7 %collective-permute-start.39 = (f32[2,16,128]{2,1,0:T(8,128)S(1)}, f32[2,16,128]{2,1,0:T(8,128)S(1)}, u32[]{:S(2)}, u32[]{:S(2)}) collective-permute-start(f32[2,16,128]{2,1,0:T(8,128)S(1)} %fusion.1), channel_id=1, source_target_pairs={{0,4},{1,5},{2,6},{3,7},{4,0},{5,1},{6,2},{7,3},{8,12},{9,13},{10,... | collective-permute-start | bytes 49160 | tf_op jit(solution)/shard_map/exchange/ppermute | solution.py:38
  212.7 5.3 %collective-permute-start.40 = (f32[2,16,128]{2,1,0:T(8,128)S(1)}, f32[2,16,128]{2,1,0:T(8,128)S(1)}, u32[]{:S(2)}, u32[]{:S(2)}) collective-permute-start(f32[2,16,128]{2,1,0:T(8,128)S(1)} %add.41), channel_id=1, source_target_pairs={{0,8},{1,9},{2,10},{3,11},{4,12},{5,13},{6,14},{7,15},{8,0},{9,1},... | collective-permute-start | bytes 49160 | tf_op jit(solution)/shard_map/exchange/ppermute | solution.py:38

commit v2 on v1

--- a/solution.py
+++ b/solution.py
@@ -331,7 +331,7 @@
         else:
             coeffs(i)
             fit(i - 1, [blocks[i][0]])
-    fit(last, arrived[last - 1][1:3] if last else [])
+    fit(last, arrived[last - 1][1:2] if last else [])
 
     with jax.named_scope("fitted_out"):
         fitted = call(
@@ -353,6 +353,7 @@
             [SMEM] + [VMEM] * len(pieces),
             "exchange",
             (spot, *pieces),
+            [fitted],
             scratch=[pltpu.VMEM((128, 128), F32)] + [pltpu.VMEM((2048, 128), F32)] * 4,
             flops=2 * 128 * 128 * 4096,
             nbytes=2 << 20,

time: 219 us -> 217 us (level)
  waiting for transfers between devices: 138 us -> 133 us
    ppermute x33, waiting for transfers between devices: 122 us -> 119 us  [move(): return lax.ppermute(value, ('row', 'col'), pairs)]
    ppermute x4, waiting for transfers between devices: 4.18 us -> 1.52 us  [swap_core(): return lax.ppermute(value, 'row', [(r, r ^ 1) for r in range(8)])]
  transfers between devices with their start and end apart: 41 -> 41, of which waited for: 28 -> 27; matrix products, arithmetic and copies ran while one was open for 0% -> 1% of each run, Pallas kernels for 7% -> 7%
where the time goes in v2:
time: 217 us
  waiting for transfers between devices  133 us (61%)
  starting transfers between devices  49.7 us (23%)
  Pallas kernels  27.7 us (13%)
  local copies, waits for them, and re-layouts  3.09 us (1%)
  between operations  2.45 us (1%)
    ppermute x33, waiting for transfers between devices, move(): return lax.ppermute(value, ('row', 'col'), pairs)  119 us
    ppermute x33, starting transfers between devices, move(): return lax.ppermute(value, ('row', 'col'), pairs)  44.2 us
    pallas_call x21, Pallas kernels, call(): pl.pallas_call(kernel, out_shape=out_shape, in_specs=list(in_specs) + [VM...  23.5 us
    ppermute x4, waiting for transfers between devices, trade(): return lax.ppermute(value, 'col', pairs)  12.8 us
    ppermute x4, starting transfers between devices, trade(): return lax.ppermute(value, 'col', pairs)  5.24 us
  transfers between devices with their start and end apart: 41, of which 27 were waited for; matrix products, arithmetic and copies ran while one was open for 1% of the time, Pallas kernels for 7%

profile of v2, /device:TPU:6, one launch (start us, length us, event | category | flops | bytes accessed | tf_op | source)
XLA Modules:
  0.0 216.7 jit_solution(7544687534006444082)
XLA Ops:
  2.0 1.6 copy-done.1
  3.6 1.9 relayout.2.refs_0_
  5.7 1.6 collective-permute-start
  7.4 2.9 %collective-permute-start.1 = (bf16[65,16,128]{2,1,0:T(8,128)(2,1)S(1)}, bf16[65,16,128]{2,1,0:T(8,128)(2,1)S(1)}, u32[]{:S(2)}, u32[]{:S(2)}) collective-permute-start(bf16[65,16,128]{2,1,0:T(8,128)(2,1)S(1)} %get-tuple-element.58), channel_id=1, source_target_pairs={{0,2},{1,3},{2,0},{3,1},{4,6},{5,7},{6,4},{7,5},{8,10},{9,11},{10,... | collective-permute-start | bytes 798728 | tf_op jit(solution)/shard_map/tiles_over_y/ppermute | solution.py:33
  10.3 1.3 collective-permute-start.2
  11.6 2.3 %relayout.3.refs_0_ = bf16[4,193,16,128]{3,2,1,0:T(8,128)(2,1)S(1)} custom-call(s32[5]{0:T(128)S(1)} %stack.37.spot_ref.refs_0_, bf16[64,128,128]{2,1,0:T(8,128)(2,1)S(1)} %bitcast.54, bf16[1024,256]{1,0:T(8,128)(2,1)S(1)} %copy-done), custom_call_target="tpu_custom_call" | custom-call | bytes 4194304 | tf_op jit(solution)/shard_map/relayout/pallas_call | solution.py:99
  13.9 2.2 %collective-permute-done.refs_1_ = bf16[65,16,128]{2,1,0:T(8,128)(2,1)S(1)} collective-permute-done((bf16[65,16,128]{2,1,0:T(8,128)(2,1)S(1)}, bf16[65,16,128]{2,1,0:T(8,128)(2,1)S(1)}, u32[]{:S(2)}, u32[]{:S(2)}) %collective-permute-start) | collective-permute-done | bytes 266272 | tf_op jit(solution)/shard_map/tiles_over_y/ppermute | solution.py:33
  16.1 6.5 %collective-permute-done.1.refs_2_ = bf16[65,16,128]{2,1,0:T(8,128)(2,1)S(1)} collective-permute-done((bf16[65,16,128]{2,1,0:T(8,128)(2,1)S(1)}, bf16[65,16,128]{2,1,0:T(8,128)(2,1)S(1)}, u32[]{:S(2)}, u32[]{:S(2)}) %collective-permute-start.1) | collective-permute-done | bytes 266272 | tf_op jit(solution)/shard_map/tiles_over_y/ppermute | solution.py:33
  22.7 2.0 collective-permute-start.3
  25.3 1.3 collective-permute-start.4
  26.6 10.8 %collective-permute-done.4.refs_3_.refs_8_ = bf16[193,16,128]{2,1,0:T(8,128)(2,1)S(1)} collective-permute-done((bf16[193,16,128]{2,1,0:T(8,128)(2,1)S(1)}, bf16[193,16,128]{2,1,0:T(8,128)(2,1)S(1)}, u32[]{:S(2)}, u32[]{:S(2)}) %collective-permute-start.4) | collective-permute-done | bytes 790560 | tf_op jit(solution)/shard_map/tiles_over_y/ppermute | solution.py:33
  37.4 2.3 %collective-permute-done.3.refs_0_ = bf16[4,1040,128]{2,1,0:T(8,128)(2,1)S(1)} collective-permute-done((bf16[4,1040,128]{2,1,0:T(8,128)(2,1)S(1)}, bf16[4,1040,128]{2,1,0:T(8,128)(2,1)S(1)}, u32[]{:S(2)}, u32[]{:S(2)}) %collective-permute-start.3) | collective-permute-done | bytes 1064992 | tf_op jit(solution)/shard_map/tiles_over_z/ppermute | solution.py:33
  39.9 2.1 collective-permute-start.5
  42.0 2.7 %collective-permute-start.8 = (bf16[193,16,128]{2,1,0:T(8,128)(2,1)S(1)}, bf16[193,16,128]{2,1,0:T(8,128)(2,1)S(1)}, u32[]{:S(2)}, u32[]{:S(2)}) collective-permute-start(bf16[193,16,128]{2,1,0:T(8,128)(2,1)S(1)} %get-tuple-element.54), channel_id=1, source_target_pairs={{0,2},{1,3},{2,0},{3,1},{4,6},{5,7},{6,4},{7,5},{8,10},{9,11},{10,... | collective-permute-start | bytes 2371592 | tf_op jit(solution)/shard_map/tiles_over_y/ppermute | solution.py:33
  44.7 19.8 %collective-permute-done.5.refs_3_ = bf16[4,1040,128]{2,1,0:T(8,128)(2,1)S(1)} collective-permute-done((bf16[4,1040,128]{2,1,0:T(8,128)(2,1)S(1)}, bf16[4,1040,128]{2,1,0:T(8,128)(2,1)S(1)}, u32[]{:S(2)}, u32[]{:S(2)}) %collective-permute-start.5) | collective-permute-done | bytes 1064992 | tf_op jit(solution)/shard_map/tiles_over_z/ppermute | solution.py:33
  65.3 6.9 %collective-permute-done.7.refs_1_.refs_6_ = bf16[193,16,128]{2,1,0:T(8,128)(2,1)S(1)} collective-permute-done((bf16[193,16,128]{2,1,0:T(8,128)(2,1)S(1)}, bf16[193,16,128]{2,1,0:T(8,128)(2,1)S(1)}, u32[]{:S(2)}, u32[]{:S(2)}) %collective-permute-start.7) | collective-permute-done | bytes 790560 | tf_op jit(solution)/shard_map/tiles_over_y/ppermute | solution.py:33
  72.3 3.8 %product.4 = bf16[4,4,2,128,256]{4,3,2,1,0:T(8,128)(2,1)S(1)} custom-call(s32[5]{0:T(128)S(1)} %stack.37.spot_ref.refs_0_, bf16[4,1040,128]{2,1,0:T(8,128)(2,1)S(1)} %stack.43.refs_0_.refs_1_, bf16[4,1040,128]{2,1,0:T(8,128)(2,1)S(1)} %gate.6.refs_2_, bf16[4,1040,128]{2,1,0:T(8,128)(2,1)S(1)} %collective-permute-done.5.refs_3_, ...), custom_call_target="tpu_custom_call" | custom-call | flops 2147483648 | bytes 6291456 | tf_op jit(solution)/shard_map/products/product/pallas_call | solution.py:51
  76.3 3.8 %product.5.refs_0_ = bf16[4,4,2,128,256]{4,3,2,1,0:T(8,128)(2,1)S(1)} custom-call(s32[5]{0:T(128)S(1)} %stack.37.spot_ref.refs_0_, bf16[4,1040,128]{2,1,0:T(8,128)(2,1)S(1)} %stack.43.refs_0_.refs_1_, bf16[4,1040,128]{2,1,0:T(8,128)(2,1)S(1)} %gate.6.refs_2_, bf16[4,1040,128]{2,1,0:T(8,128)(2,1)S(1)} %collective-permute-done.5.refs_3_, ...), custom_call_target="tpu_custom_call" | custom-call | flops 2147483648 | bytes 6291456 | tf_op jit(solution)/shard_map/products/product/pallas_call | solution.py:51
  80.0 12.4 %collective-permute-done.10.refs_0_ = bf16[4,1040,128]{2,1,0:T(8,128)(2,1)S(1)} collective-permute-done((bf16[4,1040,128]{2,1,0:T(8,128)(2,1)S(1)}, bf16[4,1040,128]{2,1,0:T(8,128)(2,1)S(1)}, u32[]{:S(2)}, u32[]{:S(2)}) %collective-permute-start.10) | collective-permute-done | bytes 1064992 | tf_op jit(solution)/shard_map/tiles_over_z/ppermute | solution.py:33
  95.6 1.6 collective-permute-start.11
  97.2 9.3 %collective-permute-done.12.refs_2_ = bf16[4,2,128,256]{3,2,1,0:T(8,128)(2,1)S(1)} collective-permute-done((bf16[4,2,128,256]{3,2,1,0:T(8,128)(2,1)S(1)}, bf16[4,2,128,256]{3,2,1,0:T(8,128)(2,1)S(1)}, u32[]{:S(2)}, u32[]{:S(2)}) %collective-permute-start.12) | collective-permute-done | bytes 524320 | tf_op jit(solution)/shard_map/sum_x/ppermute | solution.py:33
  107.5 8.5 %collective-permute-done.13.refs_3_ = bf16[4,2,128,256]{3,2,1,0:T(8,128)(2,1)S(1)} collective-permute-done((bf16[4,2,128,256]{3,2,1,0:T(8,128)(2,1)S(1)}, bf16[4,2,128,256]{3,2,1,0:T(8,128)(2,1)S(1)}, u32[]{:S(2)}, u32[]{:S(2)}) %collective-permute-start.13) | collective-permute-done | bytes 524320 | tf_op jit(solution)/shard_map/sum_x/ppermute | solution.py:33
  115.9 2.2 collective-permute-done.17.refs_3_
  118.8 3.7 %product.6 = bf16[4,4,2,128,256]{4,3,2,1,0:T(8,128)(2,1)S(1)} custom-call(s32[5]{0:T(128)S(1)} %stack.37.spot_ref.refs_0_, bf16[4,1040,128]{2,1,0:T(8,128)(2,1)S(1)} %stack.44.refs_0_.refs_1_, bf16[4,1040,128]{2,1,0:T(8,128)(2,1)S(1)} %gate.8.refs_2_, bf16[4,1040,128]{2,1,0:T(8,128)(2,1)S(1)} %collective-permute-done.17.refs_3_, ...), custom_call_target="tpu_custom_call" | custom-call | flops 2147483648 | bytes 6291456 | tf_op jit(solution)/shard_map/products/product/pallas_call | solution.py:51
  122.6 3.8 %product.7.refs_0_ = bf16[4,4,2,128,256]{4,3,2,1,0:T(8,128)(2,1)S(1)} custom-call(s32[5]{0:T(128)S(1)} %stack.37.spot_ref.refs_0_, bf16[4,1040,128]{2,1,0:T(8,128)(2,1)S(1)} %stack.44.refs_0_.refs_1_, bf16[4,1040,128]{2,1,0:T(8,128)(2,1)S(1)} %gate.8.refs_2_, bf16[4,1040,128]{2,1,0:T(8,128)(2,1)S(1)} %collective-permute-done.17.refs_3_, ...), custom_call_target="tpu_custom_call" | custom-call | flops 2147483648 | bytes 6291456 | tf_op jit(solution)/shard_map/products/product/pallas_call | solution.py:51
  127.0 2.5 %collective-permute-start.21 = (bf16[4,2,128,256]{3,2,1,0:T(8,128)(2,1)S(1)}, bf16[4,2,128,256]{3,2,1,0:T(8,128)(2,1)S(1)}, u32[]{:S(2)}, u32[]{:S(2)}) collective-permute-start(bf16[4,2,128,256]{3,2,1,0:T(8,128)(2,1)S(1)} %get-tuple-element.35), channel_id=1, source_target_pairs={{0,32},{1,33},{2,34},{3,35},{4,36},{5,37},{6,38},{7,39},{8,40},{9,... | collective-permute-start | bytes 1572872 | tf_op jit(solution)/shard_map/sum_x/ppermute | solution.py:33
  129.5 12.0 %collective-permute-done.21.refs_2_ = bf16[4,2,128,256]{3,2,1,0:T(8,128)(2,1)S(1)} collective-permute-done((bf16[4,2,128,256]{3,2,1,0:T(8,128)(2,1)S(1)}, bf16[4,2,128,256]{3,2,1,0:T(8,128)(2,1)S(1)}, u32[]{:S(2)}, u32[]{:S(2)}) %collective-permute-start.21) | collective-permute-done | bytes 524320 | tf_op jit(solution)/shard_map/sum_x/ppermute | solution.py:33
  141.7 3.8 %collective-permute-start.22 = (bf16[4,2,128,256]{3,2,1,0:T(8,128)(2,1)S(1)}, bf16[4,2,128,256]{3,2,1,0:T(8,128)(2,1)S(1)}, u32[]{:S(2)}, u32[]{:S(2)}) collective-permute-start(bf16[4,2,128,256]{3,2,1,0:T(8,128)(2,1)S(1)} %relay.3), channel_id=1, source_target_pairs={{0,32},{1,33},{2,34},{3,35},{4,36},{5,37},{6,38},{7,39},{8,40},{9,... | collective-permute-start | bytes 1572872 | tf_op jit(solution)/shard_map/sum_x/ppermute | solution.py:33
  146.1 1.7 collective-permute-start.16
  147.8 4.3 %collective-permute-done.22.refs_3_ = bf16[4,2,128,256]{3,2,1,0:T(8,128)(2,1)S(1)} collective-permute-done((bf16[4,2,128,256]{3,2,1,0:T(8,128)(2,1)S(1)}, bf16[4,2,128,256]{3,2,1,0:T(8,128)(2,1)S(1)}, u32[]{:S(2)}, u32[]{:S(2)}) %collective-permute-start.22) | collective-permute-done | bytes 524320 | tf_op jit(solution)/shard_map/sum_x/ppermute | solution.py:33
  152.5 1.3 collective-permute-done.16.refs_4_
  154.7 2.5 %collective-permute-start.26 = (bf16[2,2,16,2048]{3,2,1,0:T(8,128)(2,1)S(1)}, bf16[2,2,16,2048]{3,2,1,0:T(8,128)(2,1)S(1)}, u32[]{:S(2)}, u32[]{:S(2)}) collective-permute-start(bf16[2,2,16,2048]{3,2,1,0:T(8,128)(2,1)S(1)} %get-tuple-element.41), channel_id=1, source_target_pairs={{0,32},{1,33},{2,34},{3,35},{4,36},{5,37},{6,38},{7,39},{8,40},{9,... | collective-permute-start | bytes 786440 | tf_op jit(solution)/shard_map/exchange_over_row/ppermute | solution.py:33
  157.5 1.8 collective-permute-start.25
  159.2 7.9 %collective-permute-done.26.refs_2_ = bf16[2,2,16,2048]{3,2,1,0:T(8,128)(2,1)S(1)} collective-permute-done((bf16[2,2,16,2048]{3,2,1,0:T(8,128)(2,1)S(1)}, bf16[2,2,16,2048]{3,2,1,0:T(8,128)(2,1)S(1)}, u32[]{:S(2)}, u32[]{:S(2)}) %collective-permute-start.26) | collective-permute-done | bytes 262176 | tf_op jit(solution)/shard_map/exchange_over_row/ppermute | solution.py:33
  168.2 5.7 %collective-permute-start.30 = (bf16[2,2,16,2048]{3,2,1,0:T(8,128)(2,1)S(1)}, bf16[2,2,16,2048]{3,2,1,0:T(8,128)(2,1)S(1)}, u32[]{:S(2)}, u32[]{:S(2)}) collective-permute-start(bf16[2,2,16,2048]{3,2,1,0:T(8,128)(2,1)S(1)} %get-tuple-element.48), channel_id=1, source_target_pairs={{0,64},{1,65},{2,66},{3,67},{4,68},{5,69},{6,70},{7,71},{8,72},{9,... | collective-permute-start | bytes 786440 | tf_op jit(solution)/shard_map/exchange_over_row/ppermute | solution.py:33
  173.9 2.5 %collective-permute-start.29 = (bf16[2,2,16,2048]{3,2,1,0:T(8,128)(2,1)S(1)}, bf16[2,2,16,2048]{3,2,1,0:T(8,128)(2,1)S(1)}, u32[]{:S(2)}, u32[]{:S(2)}) collective-permute-start(bf16[2,2,16,2048]{3,2,1,0:T(8,128)(2,1)S(1)} %get-tuple-element.47), channel_id=1, source_target_pairs={{0,32},{1,33},{2,34},{3,35},{4,36},{5,37},{6,38},{7,39},{8,40},{9,... | collective-permute-start | bytes 786440 | tf_op jit(solution)/shard_map/exchange_over_row/ppermute | solution.py:33
  176.6 2.0 collective-permute-done.31.refs_8_
  178.6 4.1 %collective-permute-done.30.refs_7_ = bf16[2,2,16,2048]{3,2,1,0:T(8,128)(2,1)S(1)} collective-permute-done((bf16[2,2,16,2048]{3,2,1,0:T(8,128)(2,1)S(1)}, bf16[2,2,16,2048]{3,2,1,0:T(8,128)(2,1)S(1)}, u32[]{:S(2)}, u32[]{:S(2)}) %collective-permute-start.30) | collective-permute-done | bytes 262176 | tf_op jit(solution)/shard_map/exchange_over_row/ppermute | solution.py:33
  183.0 2.5 %assemble.1 = bf16[2,64,16,256]{3,2,1,0:T(8,128)(2,1)} custom-call(bf16[2,64,2048]{2,1,0:T(8,128)(2,1)S(1)} %get-tuple-element.37.refs_0_, bf16[2,64,2048]{2,1,0:T(8,128)(2,1)S(1)} %get-tuple-element.42.refs_1_), custom_call_target="tpu_custom_call" | custom-call | bytes 2097152 | tf_op jit(solution)/shard_map/fitted_out/assemble/pallas_call | solution.py:51
  186.2 2.0 exchange.1
  188.5 3.0 %collective-permute-start.33 = (f32[32,128]{1,0:T(8,128)S(1)}, f32[32,128]{1,0:T(8,128)S(1)}, u32[]{:S(2)}, u32[]{:S(2)}) collective-permute-start(f32[32,128]{1,0:T(8,128)S(1)} %get-tuple-element.51), channel_id=1, source_target_pairs={{0,32},{1,33},{2,34},{3,35},{4,36},{5,37},{6,38},{7,39},{8,40},{9,... | collective-permute-start | bytes 49160 | tf_op jit(solution)/shard_map/exchange/ppermute | solution.py:33
  193.3 3.5 %collective-permute-done.34 = f32[32,128]{1,0:T(8,128)S(1)} collective-permute-done((f32[32,128]{1,0:T(8,128)S(1)}, f32[32,128]{1,0:T(8,128)S(1)}, u32[]{:S(2)}, u32[]{:S(2)}) %collective-permute-start.34) | collective-permute-done | bytes 16416 | tf_op jit(solution)/shard_map/exchange/ppermute | solution.py:33
  198.1 3.7 %collective-permute-done.37 = f32[2,16,128]{2,1,0:T(8,128)S(1)} collective-permute-done((f32[2,16,128]{2,1,0:T(8,128)S(1)}, f32[2,16,128]{2,1,0:T(8,128)S(1)}, u32[]{:S(2)}, u32[]{:S(2)}) %collective-permute-start.37) | collective-permute-done | bytes 16416 | tf_op jit(solution)/shard_map/exchange/ppermute | solution.py:38
  201.9 2.1 collective-permute-start.38
  203.9 3.2 %collective-permute-done.38 = f32[2,16,128]{2,1,0:T(8,128)S(1)} collective-permute-done((f32[2,16,128]{2,1,0:T(8,128)S(1)}, f32[2,16,128]{2,1,0:T(8,128)S(1)}, u32[]{:S(2)}, u32[]{:S(2)}) %collective-permute-start.38) | collective-permute-done | bytes 16416 | tf_op jit(solution)/shard_map/exchange/ppermute | solution.py:38
  207.1 3.7 %collective-permute-done.39 = f32[2,16,128]{2,1,0:T(8,128)S(1)} collective-permute-done((f32[2,16,128]{2,1,0:T(8,128)S(1)}, f32[2,16,128]{2,1,0:T(8,128)S(1)}, u32[]{:S(2)}, u32[]{:S(2)}) %collective-permute-start.39) | collective-permute-done | bytes 16416 | tf_op jit(solution)/shard_map/exchange/ppermute | solution.py:38
  210.9 3.1 %collective-permute-start.40 = (f32[2,16,128]{2,1,0:T(8,128)S(1)}, f32[2,16,128]{2,1,0:T(8,128)S(1)}, u32[]{:S(2)}, u32[]{:S(2)}) collective-permute-start(f32[2,16,128]{2,1,0:T(8,128)S(1)} %add.41), channel_id=1, source_target_pairs={{0,8},{1,9},{2,10},{3,11},{4,12},{5,13},{6,14},{7,15},{8,0},{9,1},... | collective-permute-start | bytes 49160 | tf_op jit(solution)/shard_map/exchange/ppermute | solution.py:38
  214.0 2.1 collective-permute-done.40
  (109 shorter events, 15.9 us)
Async XLA Ops:
  2.0 1.6 copy-start.1
  3.6 8.0 %copy-start = (bf16[1024,256]{1,0:T(8,128)(2,1)S(1)}, bf16[1024,256]{1,0:T(8,128)(2,1)}, u32[]{:S(2)}) copy-start(bf16[1024,256]{1,0:T(8,128)(2,1)} %refs_5_.9) | copy-start | bytes 1572868
  3.6 8.0 %copy-start.2 = (bf16[1,64,128,128]{3,2,1,0:T(8,128)(2,1)S(1)}, bf16[1,64,128,128]{3,2,1,0:T(8,128)(2,1)}, u32[]{:S(2)}) copy-start(bf16[1,64,128,128]{3,2,1,0:T(8,128)(2,1)} %param.5) | copy-start | bytes 6291460
  5.7 10.4 %collective-permute-start = (bf16[65,16,128]{2,1,0:T(8,128)(2,1)S(1)}, bf16[65,16,128]{2,1,0:T(8,128)(2,1)S(1)}, u32[]{:S(2)}, u32[]{:S(2)}) collective-permute-start(bf16[65,16,128]{2,1,0:T(8,128)(2,1)S(1)} %get-tuple-element.59), channel_id=1, source_target_pairs={{0,1},{1,2},{2,3},{3,0},{4,5},{5,6},{6,7},{7,4},{8,9},{9,10},{10,1... | collective-permute-start | bytes 798728 | tf_op jit(solution)/shard_map/tiles_over_y/ppermute | solution.py:33
  7.4 15.2 %collective-permute-start.1 = (bf16[65,16,128]{2,1,0:T(8,128)(2,1)S(1)}, bf16[65,16,128]{2,1,0:T(8,128)(2,1)S(1)}, u32[]{:S(2)}, u32[]{:S(2)}) collective-permute-start(bf16[65,16,128]{2,1,0:T(8,128)(2,1)S(1)} %get-tuple-element.58), channel_id=1, source_target_pairs={{0,2},{1,3},{2,0},{3,1},{4,6},{5,7},{6,4},{7,5},{8,10},{9,11},{10,... | collective-permute-start | bytes 798728 | tf_op jit(solution)/shard_map/tiles_over_y/ppermute | solution.py:33
  10.3 12.3 %collective-permute-start.2 = (bf16[65,16,128]{2,1,0:T(8,128)(2,1)S(1)}, bf16[65,16,128]{2,1,0:T(8,128)(2,1)S(1)}, u32[]{:S(2)}, u32[]{:S(2)}) collective-permute-start(bf16[65,16,128]{2,1,0:T(8,128)(2,1)S(1)} %get-tuple-element.57), channel_id=1, source_target_pairs={{0,3},{1,0},{2,1},{3,2},{4,7},{5,4},{6,5},{7,6},{8,11},{9,8},{10,9... | collective-permute-start | bytes 798728 | tf_op jit(solution)/shard_map/tiles_over_y/ppermute | solution.py:33
  22.7 17.1 %collective-permute-start.3 = (bf16[4,1040,128]{2,1,0:T(8,128)(2,1)S(1)}, bf16[4,1040,128]{2,1,0:T(8,128)(2,1)S(1)}, u32[]{:S(2)}, u32[]{:S(2)}) collective-permute-start(bf16[4,1040,128]{2,1,0:T(8,128)(2,1)S(1)} %stack.43.refs_0_.refs_1_), channel_id=1, source_target_pairs={{0,4},{1,5},{2,6},{3,7},{4,8},{5,9},{6,10},{7,11},{8,12},{9,13},{1... | collective-permute-start | bytes 3194888 | tf_op jit(solution)/shard_map/tiles_over_z/ppermute | solution.py:33
  25.3 12.1 %collective-permute-start.4 = (bf16[193,16,128]{2,1,0:T(8,128)(2,1)S(1)}, bf16[193,16,128]{2,1,0:T(8,128)(2,1)S(1)}, u32[]{:S(2)}, u32[]{:S(2)}) collective-permute-start(bf16[193,16,128]{2,1,0:T(8,128)(2,1)S(1)} %get-tuple-element.56), channel_id=1, source_target_pairs={{0,3},{1,0},{2,1},{3,2},{4,7},{5,4},{6,5},{7,6},{8,11},{9,8},{10,9... | collective-permute-start | bytes 2371592 | tf_op jit(solution)/shard_map/tiles_over_y/ppermute | solution.py:33
  39.9 24.6 %collective-permute-start.5 = (bf16[4,1040,128]{2,1,0:T(8,128)(2,1)S(1)}, bf16[4,1040,128]{2,1,0:T(8,128)(2,1)S(1)}, u32[]{:S(2)}, u32[]{:S(2)}) collective-permute-start(bf16[4,1040,128]{2,1,0:T(8,128)(2,1)S(1)} %gate.7), channel_id=1, source_target_pairs={{0,12},{1,13},{2,14},{3,15},{4,0},{5,1},{6,2},{7,3},{8,4},{9,5},{1... | collective-permute-start | bytes 3194888 | tf_op jit(solution)/shard_map/tiles_over_z/ppermute | solution.py:33
  42.0 23.3 %collective-permute-start.6 = (bf16[4,1040,128]{2,1,0:T(8,128)(2,1)S(1)}, bf16[4,1040,128]{2,1,0:T(8,128)(2,1)S(1)}, u32[]{:S(2)}, u32[]{:S(2)}) collective-permute-start(bf16[4,1040,128]{2,1,0:T(8,128)(2,1)S(1)} %gate.6.refs_2_), channel_id=1, source_target_pairs={{0,4},{1,5},{2,6},{3,7},{4,8},{5,9},{6,10},{7,11},{8,12},{9,13},{1... | collective-permute-start | bytes 3194888 | tf_op jit(solution)/shard_map/tiles_over_z/ppermute | solution.py:33
  42.0 30.2 %collective-permute-start.7 = (bf16[193,16,128]{2,1,0:T(8,128)(2,1)S(1)}, bf16[193,16,128]{2,1,0:T(8,128)(2,1)S(1)}, u32[]{:S(2)}, u32[]{:S(2)}) collective-permute-start(bf16[193,16,128]{2,1,0:T(8,128)(2,1)S(1)} %get-tuple-element.55), channel_id=1, source_target_pairs={{0,1},{1,2},{2,3},{3,0},{4,5},{5,6},{6,7},{7,4},{8,9},{9,10},{10,1... | collective-permute-start | bytes 2371592 | tf_op jit(solution)/shard_map/tiles_over_y/ppermute | solution.py:33
  42.0 30.2 %collective-permute-start.8 = (bf16[193,16,128]{2,1,0:T(8,128)(2,1)S(1)}, bf16[193,16,128]{2,1,0:T(8,128)(2,1)S(1)}, u32[]{:S(2)}, u32[]{:S(2)}) collective-permute-start(bf16[193,16,128]{2,1,0:T(8,128)(2,1)S(1)} %get-tuple-element.54), channel_id=1, source_target_pairs={{0,2},{1,3},{2,0},{3,1},{4,6},{5,7},{6,4},{7,5},{8,10},{9,11},{10,... | collective-permute-start | bytes 2371592 | tf_op jit(solution)/shard_map/tiles_over_y/ppermute | solution.py:33
  76.1 16.4 %collective-permute-start.9 = (bf16[4,4,2,128,256]{4,3,2,1,0:T(8,128)(2,1)S(1)}, bf16[4,4,2,128,256]{4,3,2,1,0:T(8,128)(2,1)S(1)}, u32[]{:S(2)}, u32[]{:S(2)}) collective-permute-start(bf16[4,4,2,128,256]{4,3,2,1,0:T(8,128)(2,1)S(1)} %product.4), channel_id=1, source_target_pairs={{0,16},{16,0},{32,48},{48,32},{64,80},{80,64},{96,112},{112,96},{1... | collective-permute-start | bytes 6291464 | tf_op jit(solution)/shard_map/sum_cores/ppermute | solution.py:42
  76.1 16.3 %collective-permute-start.10 = (bf16[4,1040,128]{2,1,0:T(8,128)(2,1)S(1)}, bf16[4,1040,128]{2,1,0:T(8,128)(2,1)S(1)}, u32[]{:S(2)}, u32[]{:S(2)}) collective-permute-start(bf16[4,1040,128]{2,1,0:T(8,128)(2,1)S(1)} %stack.44.refs_0_.refs_1_), channel_id=1, source_target_pairs={{0,4},{1,5},{2,6},{3,7},{4,8},{5,9},{6,10},{7,11},{8,12},{9,13},{1... | collective-permute-start | bytes 3194888 | tf_op jit(solution)/shard_map/tiles_over_z/ppermute | solution.py:33
  92.7 13.7 %collective-permute-start.12 = (bf16[4,2,128,256]{3,2,1,0:T(8,128)(2,1)S(1)}, bf16[4,2,128,256]{3,2,1,0:T(8,128)(2,1)S(1)}, u32[]{:S(2)}, u32[]{:S(2)}) collective-permute-start(bf16[4,2,128,256]{3,2,1,0:T(8,128)(2,1)S(1)} %get-tuple-element.29), channel_id=1, source_target_pairs={{0,32},{1,33},{2,34},{3,35},{4,36},{5,37},{6,38},{7,39},{8,40},{9,... | collective-permute-start | bytes 1572872 | tf_op jit(solution)/shard_map/sum_x/ppermute | solution.py:33
  93.4 24.7 %collective-permute-start.17 = (bf16[4,1040,128]{2,1,0:T(8,128)(2,1)S(1)}, bf16[4,1040,128]{2,1,0:T(8,128)(2,1)S(1)}, u32[]{:S(2)}, u32[]{:S(2)}) collective-permute-start(bf16[4,1040,128]{2,1,0:T(8,128)(2,1)S(1)} %gate.9), channel_id=1, source_target_pairs={{0,12},{1,13},{2,14},{3,15},{4,0},{5,1},{6,2},{7,3},{8,4},{9,5},{1... | collective-permute-start | bytes 3194888 | tf_op jit(solution)/shard_map/tiles_over_z/ppermute | solution.py:33
  94.5 24.2 %collective-permute-start.18 = (bf16[4,1040,128]{2,1,0:T(8,128)(2,1)S(1)}, bf16[4,1040,128]{2,1,0:T(8,128)(2,1)S(1)}, u32[]{:S(2)}, u32[]{:S(2)}) collective-permute-start(bf16[4,1040,128]{2,1,0:T(8,128)(2,1)S(1)} %gate.8.refs_2_), channel_id=1, source_target_pairs={{0,4},{1,5},{2,6},{3,7},{4,8},{5,9},{6,10},{7,11},{8,12},{9,13},{1... | collective-permute-start | bytes 3194888 | tf_op jit(solution)/shard_map/tiles_over_z/ppermute | solution.py:33
  95.6 11.8 %collective-permute-start.11 = (bf16[4,2,128,256]{3,2,1,0:T(8,128)(2,1)S(1)}, bf16[4,2,128,256]{3,2,1,0:T(8,128)(2,1)S(1)}, u32[]{:S(2)}, u32[]{:S(2)}) collective-permute-start(bf16[4,2,128,256]{3,2,1,0:T(8,128)(2,1)S(1)} %get-tuple-element.28), channel_id=1, source_target_pairs={{0,96},{1,97},{2,98},{3,99},{4,100},{5,101},{6,102},{7,103},{8,104... | collective-permute-start | bytes 1572872 | tf_op jit(solution)/shard_map/sum_x/ppermute | solution.py:33
  106.7 9.2 %collective-permute-start.13 = (bf16[4,2,128,256]{3,2,1,0:T(8,128)(2,1)S(1)}, bf16[4,2,128,256]{3,2,1,0:T(8,128)(2,1)S(1)}, u32[]{:S(2)}, u32[]{:S(2)}) collective-permute-start(bf16[4,2,128,256]{3,2,1,0:T(8,128)(2,1)S(1)} %relay.2), channel_id=1, source_target_pairs={{0,32},{1,33},{2,34},{3,35},{4,36},{5,37},{6,38},{7,39},{8,40},{9,... | collective-permute-start | bytes 1572872 | tf_op jit(solution)/shard_map/sum_x/ppermute | solution.py:33
  122.5 4.2 %collective-permute-start.19 = (bf16[4,4,2,128,256]{4,3,2,1,0:T(8,128)(2,1)S(1)}, bf16[4,4,2,128,256]{4,3,2,1,0:T(8,128)(2,1)S(1)}, u32[]{:S(2)}, u32[]{:S(2)}) collective-permute-start(bf16[4,4,2,128,256]{4,3,2,1,0:T(8,128)(2,1)S(1)} %product.6), channel_id=1, source_target_pairs={{0,16},{16,0},{32,48},{48,32},{64,80},{80,64},{96,112},{112,96},{1... | collective-permute-start | bytes 6291464 | tf_op jit(solution)/shard_map/sum_cores/ppermute | solution.py:42
  127.0 14.5 %collective-permute-start.21 = (bf16[4,2,128,256]{3,2,1,0:T(8,128)(2,1)S(1)}, bf16[4,2,128,256]{3,2,1,0:T(8,128)(2,1)S(1)}, u32[]{:S(2)}, u32[]{:S(2)}) collective-permute-start(bf16[4,2,128,256]{3,2,1,0:T(8,128)(2,1)S(1)} %get-tuple-element.35), channel_id=1, source_target_pairs={{0,32},{1,33},{2,34},{3,35},{4,36},{5,37},{6,38},{7,39},{8,40},{9,... | collective-permute-start | bytes 1572872 | tf_op jit(solution)/shard_map/sum_x/ppermute | solution.py:33
  129.5 18.3 %collective-permute-start.20 = (bf16[4,2,128,256]{3,2,1,0:T(8,128)(2,1)S(1)}, bf16[4,2,128,256]{3,2,1,0:T(8,128)(2,1)S(1)}, u32[]{:S(2)}, u32[]{:S(2)}) collective-permute-start(bf16[4,2,128,256]{3,2,1,0:T(8,128)(2,1)S(1)} %get-tuple-element.34), channel_id=1, source_target_pairs={{0,96},{1,97},{2,98},{3,99},{4,100},{5,101},{6,102},{7,103},{8,104... | collective-permute-start | bytes 1572872 | tf_op jit(solution)/shard_map/sum_x/ppermute | solution.py:33
  141.7 10.5 %collective-permute-start.22 = (bf16[4,2,128,256]{3,2,1,0:T(8,128)(2,1)S(1)}, bf16[4,2,128,256]{3,2,1,0:T(8,128)(2,1)S(1)}, u32[]{:S(2)}, u32[]{:S(2)}) collective-permute-start(bf16[4,2,128,256]{3,2,1,0:T(8,128)(2,1)S(1)} %relay.3), channel_id=1, source_target_pairs={{0,32},{1,33},{2,34},{3,35},{4,36},{5,37},{6,38},{7,39},{8,40},{9,... | collective-permute-start | bytes 1572872 | tf_op jit(solution)/shard_map/sum_x/ppermute | solution.py:33
  145.7 6.7 %collective-permute-start.14 = (bf16[2,128,256]{2,1,0:T(8,128)(2,1)S(1)}, bf16[2,128,256]{2,1,0:T(8,128)(2,1)S(1)}, u32[]{:S(2)}, u32[]{:S(2)}) collective-permute-start(bf16[2,128,256]{2,1,0:T(8,128)(2,1)S(1)} %get-tuple-element.31), channel_id=1, source_target_pairs={{0,3},{1,0},{2,1},{3,2},{4,7},{5,4},{6,5},{7,6},{8,11},{9,8},{10,9... | collective-permute-start | bytes 393224 | tf_op jit(solution)/shard_map/coeffs_over_y/ppermute | solution.py:33
  145.8 6.7 %collective-permute-start.15 = (bf16[2,128,256]{2,1,0:T(8,128)(2,1)S(1)}, bf16[2,128,256]{2,1,0:T(8,128)(2,1)S(1)}, u32[]{:S(2)}, u32[]{:S(2)}) collective-permute-start(bf16[2,128,256]{2,1,0:T(8,128)(2,1)S(1)} %get-tuple-element.32), channel_id=1, source_target_pairs={{0,2},{1,3},{2,0},{3,1},{4,6},{5,7},{6,4},{7,5},{8,10},{9,11},{10,... | collective-permute-start | bytes 393224 | tf_op jit(solution)/shard_map/coeffs_over_y/ppermute | solution.py:33
  146.1 7.7 %copy-start.3 = (f32[2,64,64]{2,1,0:T(8,128)S(1)}, f32[2,64,64]{2,1,0:T(8,128)}, u32[]{:S(2)}) copy-start(f32[2,64,64]{2,1,0:T(8,128)} %refs_5_.11) | copy-start | bytes 98308
  146.1 7.7 %collective-permute-start.16 = (bf16[2,128,256]{2,1,0:T(8,128)(2,1)S(1)}, bf16[2,128,256]{2,1,0:T(8,128)(2,1)S(1)}, u32[]{:S(2)}, u32[]{:S(2)}) collective-permute-start(bf16[2,128,256]{2,1,0:T(8,128)(2,1)S(1)} %get-tuple-element.33), channel_id=1, source_target_pairs={{0,1},{1,2},{2,3},{3,0},{4,5},{5,6},{6,7},{7,4},{8,9},{9,10},{10,1... | collective-permute-start | bytes 393224 | tf_op jit(solution)/shard_map/coeffs_over_y/ppermute | solution.py:33
  154.7 12.4 %collective-permute-start.26 = (bf16[2,2,16,2048]{3,2,1,0:T(8,128)(2,1)S(1)}, bf16[2,2,16,2048]{3,2,1,0:T(8,128)(2,1)S(1)}, u32[]{:S(2)}, u32[]{:S(2)}) collective-permute-start(bf16[2,2,16,2048]{3,2,1,0:T(8,128)(2,1)S(1)} %get-tuple-element.41), channel_id=1, source_target_pairs={{0,32},{1,33},{2,34},{3,35},{4,36},{5,37},{6,38},{7,39},{8,40},{9,... | collective-permute-start | bytes 786440 | tf_op jit(solution)/shard_map/exchange_over_row/ppermute | solution.py:33
  157.2 9.9 %collective-permute-start.23 = (bf16[2,128,256]{2,1,0:T(8,128)(2,1)S(1)}, bf16[2,128,256]{2,1,0:T(8,128)(2,1)S(1)}, u32[]{:S(2)}, u32[]{:S(2)}) collective-permute-start(bf16[2,128,256]{2,1,0:T(8,128)(2,1)S(1)} %get-tuple-element.38), channel_id=1, source_target_pairs={{0,3},{1,0},{2,1},{3,2},{4,7},{5,4},{6,5},{7,6},{8,11},{9,8},{10,9... | collective-permute-start | bytes 393224 | tf_op jit(solution)/shard_map/coeffs_over_y/ppermute | solution.py:33
  157.2 9.9 %collective-permute-start.24 = (bf16[2,128,256]{2,1,0:T(8,128)(2,1)S(1)}, bf16[2,128,256]{2,1,0:T(8,128)(2,1)S(1)}, u32[]{:S(2)}, u32[]{:S(2)}) collective-permute-start(bf16[2,128,256]{2,1,0:T(8,128)(2,1)S(1)} %get-tuple-element.39), channel_id=1, source_target_pairs={{0,2},{1,3},{2,0},{3,1},{4,6},{5,7},{6,4},{7,5},{8,10},{9,11},{10,... | collective-permute-start | bytes 393224 | tf_op jit(solution)/shard_map/coeffs_over_y/ppermute | solution.py:33
  157.5 9.7 %collective-permute-start.25 = (bf16[2,128,256]{2,1,0:T(8,128)(2,1)S(1)}, bf16[2,128,256]{2,1,0:T(8,128)(2,1)S(1)}, u32[]{:S(2)}, u32[]{:S(2)}) collective-permute-start(bf16[2,128,256]{2,1,0:T(8,128)(2,1)S(1)} %get-tuple-element.40), channel_id=1, source_target_pairs={{0,1},{1,2},{2,3},{3,0},{4,5},{5,6},{6,7},{7,4},{8,9},{9,10},{10,1... | collective-permute-start | bytes 393224 | tf_op jit(solution)/shard_map/coeffs_over_y/ppermute | solution.py:33
  159.2 17.3 %collective-permute-start.27 = (bf16[2,2,16,2048]{3,2,1,0:T(8,128)(2,1)S(1)}, bf16[2,2,16,2048]{3,2,1,0:T(8,128)(2,1)S(1)}, u32[]{:S(2)}, u32[]{:S(2)}) collective-permute-start(bf16[2,2,16,2048]{3,2,1,0:T(8,128)(2,1)S(1)} %get-tuple-element.44), channel_id=1, source_target_pairs={{0,64},{1,65},{2,66},{3,67},{4,68},{5,69},{6,70},{7,71},{8,72},{9,... | collective-permute-start | bytes 786440 | tf_op jit(solution)/shard_map/exchange_over_row/ppermute | solution.py:33
  167.1 9.4 %collective-permute-start.28 = (bf16[2,2,16,2048]{3,2,1,0:T(8,128)(2,1)S(1)}, bf16[2,2,16,2048]{3,2,1,0:T(8,128)(2,1)S(1)}, u32[]{:S(2)}, u32[]{:S(2)}) collective-permute-start(bf16[2,2,16,2048]{3,2,1,0:T(8,128)(2,1)S(1)} %get-tuple-element.45), channel_id=1, source_target_pairs={{0,96},{1,97},{2,98},{3,99},{4,100},{5,101},{6,102},{7,103},{8,104... | collective-permute-start | bytes 786440 | tf_op jit(solution)/shard_map/exchange_over_row/ppermute | solution.py:33
  168.1 10.5 %collective-permute-start.31 = (bf16[2,2,16,2048]{3,2,1,0:T(8,128)(2,1)S(1)}, bf16[2,2,16,2048]{3,2,1,0:T(8,128)(2,1)S(1)}, u32[]{:S(2)}, u32[]{:S(2)}) collective-permute-start(bf16[2,2,16,2048]{3,2,1,0:T(8,128)(2,1)S(1)} %get-tuple-element.49), channel_id=1, source_target_pairs={{0,96},{1,97},{2,98},{3,99},{4,100},{5,101},{6,102},{7,103},{8,104... | collective-permute-start | bytes 786440 | tf_op jit(solution)/shard_map/exchange_over_row/ppermute | solution.py:33
  168.2 14.5 %collective-permute-start.30 = (bf16[2,2,16,2048]{3,2,1,0:T(8,128)(2,1)S(1)}, bf16[2,2,16,2048]{3,2,1,0:T(8,128)(2,1)S(1)}, u32[]{:S(2)}, u32[]{:S(2)}) collective-permute-start(bf16[2,2,16,2048]{3,2,1,0:T(8,128)(2,1)S(1)} %get-tuple-element.48), channel_id=1, source_target_pairs={{0,64},{1,65},{2,66},{3,67},{4,68},{5,69},{6,70},{7,71},{8,72},{9,... | collective-permute-start | bytes 786440 | tf_op jit(solution)/shard_map/exchange_over_row/ppermute | solution.py:33
  173.9 8.8 %collective-permute-start.29 = (bf16[2,2,16,2048]{3,2,1,0:T(8,128)(2,1)S(1)}, bf16[2,2,16,2048]{3,2,1,0:T(8,128)(2,1)S(1)}, u32[]{:S(2)}, u32[]{:S(2)}) collective-permute-start(bf16[2,2,16,2048]{3,2,1,0:T(8,128)(2,1)S(1)} %get-tuple-element.47), channel_id=1, source_target_pairs={{0,32},{1,33},{2,34},{3,35},{4,36},{5,37},{6,38},{7,39},{8,40},{9,... | collective-permute-start | bytes 786440 | tf_op jit(solution)/shard_map/exchange_over_row/ppermute | solution.py:33
  182.9 3.3 %collective-permute-start.32 = (bf16[4,2,16,4096]{3,2,1,0:T(8,128)(2,1)S(1)}, bf16[4,2,16,4096]{3,2,1,0:T(8,128)(2,1)S(1)}, u32[]{:S(2)}, u32[]{:S(2)}) collective-permute-start(bf16[4,2,16,4096]{3,2,1,0:T(8,128)(2,1)S(1)} %maximum_maximum_fusion), channel_id=1, source_target_pairs={{0,16},{16,0},{32,48},{48,32},{64,80},{80,64},{96,112},{112,96},{1... | collective-permute-start | bytes 3145736 | tf_op jit(solution)/shard_map/exchange/ppermute | solution.py:42
  188.2 5.0 %collective-permute-start.35 = (f32[32,128]{1,0:T(8,128)S(1)}, f32[32,128]{1,0:T(8,128)S(1)}, u32[]{:S(2)}, u32[]{:S(2)}) collective-permute-start(f32[32,128]{1,0:T(8,128)S(1)} %get-tuple-element.53), channel_id=1, source_target_pairs={{0,96},{1,97},{2,98},{3,99},{4,100},{5,101},{6,102},{7,103},{8,104... | collective-permute-start | bytes 49160 | tf_op jit(solution)/shard_map/exchange/ppermute | solution.py:33
  188.5 4.7 %collective-permute-start.33 = (f32[32,128]{1,0:T(8,128)S(1)}, f32[32,128]{1,0:T(8,128)S(1)}, u32[]{:S(2)}, u32[]{:S(2)}) collective-permute-start(f32[32,128]{1,0:T(8,128)S(1)} %get-tuple-element.51), channel_id=1, source_target_pairs={{0,32},{1,33},{2,34},{3,35},{4,36},{5,37},{6,38},{7,39},{8,40},{9,... | collective-permute-start | bytes 49160 | tf_op jit(solution)/shard_map/exchange/ppermute | solution.py:33
  191.5 5.2 %collective-permute-start.34 = (f32[32,128]{1,0:T(8,128)S(1)}, f32[32,128]{1,0:T(8,128)S(1)}, u32[]{:S(2)}, u32[]{:S(2)}) collective-permute-start(f32[32,128]{1,0:T(8,128)S(1)} %get-tuple-element.52), channel_id=1, source_target_pairs={{0,64},{1,65},{2,66},{3,67},{4,68},{5,69},{6,70},{7,71},{8,72},{9,... | collective-permute-start | bytes 49160 | tf_op jit(solution)/shard_map/exchange/ppermute | solution.py:33
  196.8 1.3 collective-permute-start.36
  198.1 3.8 %collective-permute-start.37 = (f32[2,16,128]{2,1,0:T(8,128)S(1)}, f32[2,16,128]{2,1,0:T(8,128)S(1)}, u32[]{:S(2)}, u32[]{:S(2)}) collective-permute-start(f32[2,16,128]{2,1,0:T(8,128)S(1)} %pad_maximum_fusion), channel_id=1, source_target_pairs={{0,1},{1,0},{2,3},{3,2},{4,5},{5,4},{6,7},{7,6},{8,9},{9,8},{10,11... | collective-permute-start | bytes 49160 | tf_op jit(solution)/shard_map/exchange/ppermute | solution.py:38
  201.9 5.2 %collective-permute-start.38 = (f32[2,16,128]{2,1,0:T(8,128)S(1)}, f32[2,16,128]{2,1,0:T(8,128)S(1)}, u32[]{:S(2)}, u32[]{:S(2)}) collective-permute-start(f32[2,16,128]{2,1,0:T(8,128)S(1)} %fusion), channel_id=1, source_target_pairs={{0,2},{1,3},{2,0},{3,1},{4,6},{5,7},{6,4},{7,5},{8,10},{9,11},{10,... | collective-permute-start | bytes 49160 | tf_op jit(solution)/shard_map/exchange/ppermute | solution.py:38
  207.1 3.7 %collective-permute-start.39 = (f32[2,16,128]{2,1,0:T(8,128)S(1)}, f32[2,16,128]{2,1,0:T(8,128)S(1)}, u32[]{:S(2)}, u32[]{:S(2)}) collective-permute-start(f32[2,16,128]{2,1,0:T(8,128)S(1)} %fusion.1), channel_id=1, source_target_pairs={{0,4},{1,5},{2,6},{3,7},{4,0},{5,1},{6,2},{7,3},{8,12},{9,13},{10,... | collective-permute-start | bytes 49160 | tf_op jit(solution)/shard_map/exchange/ppermute | solution.py:38
  210.9 5.2 %collective-permute-start.40 = (f32[2,16,128]{2,1,0:T(8,128)S(1)}, f32[2,16,128]{2,1,0:T(8,128)S(1)}, u32[]{:S(2)}, u32[]{:S(2)}) collective-permute-start(f32[2,16,128]{2,1,0:T(8,128)S(1)} %add.41), channel_id=1, source_target_pairs={{0,8},{1,9},{2,10},{3,11},{4,12},{5,13},{6,14},{7,15},{8,0},{9,1},... | collective-permute-start | bytes 49160 | tf_op jit(solution)/shard_map/exchange/ppermute | solution.py:38
